TPU v7x, 128 devices: a whole 4x4x4 slice. The times are simulated.
128 devices in a mesh: section: 2 (over z_lo), fsdp: 8 (over y, core), replica: 8 (over x, z_hi).
Axes of the slice: x: 4, y: 4, z: 4 (z_hi: 2, z_lo: 2; z = z_hi * 2 + z_lo), core: 2. Of those that a mesh axis runs over, the one named last changes fastest.
Arguments:
- ends_in: bfloat16 [2, 16384, 1024], P('section', ('fsdp', 'replica')), may hold values from -6 to 6
- segment_ids: int32 [16384], P(('fsdp', 'replica')), may hold values from 0 to 15, as said below
- w_qkv: bfloat16 [2, 1024, 3072], P('section', 'fsdp'), may hold values from -0.1875 to 0.1875
- w_out: bfloat16 [2, 1024, 1024], P('section', 'fsdp'), may hold values from -0.375 to 0.375
- w_in: bfloat16 [2, 1024, 4096], P('section', 'fsdp'), may hold values from -0.1875 to 0.1875
- w_down: bfloat16 [2, 4096, 1024], P('section', 'fsdp'), may hold values from -0.09375 to 0.09375
- biases: bfloat16 [2, 6, 1024], P('section', None, 'fsdp'), may hold values from -3 to 3
- gains: bfloat16 [2, 2, 1024], P('section', None, 'fsdp'), may hold values from 0.5 to 1.5
- bias_in: bfloat16 [2, 4096], P('section', 'fsdp'), may hold values from -3 to 3
Outputs:
- ends_out: bfloat16 [2, 16384, 1024], P('section', ('fsdp', 'replica'))
- grad_qkv: float32 [2, 1024, 3072], P('section', 'fsdp')
- grad_out: float32 [2, 1024, 1024], P('section', 'fsdp')
- grad_in: float32 [2, 1024, 4096], P('section', 'fsdp')
- grad_down: float32 [2, 4096, 1024], P('section', 'fsdp')
- grad_biases: float32 [2, 6, 1024], P('section', None, 'fsdp')
- grad_gains: float32 [2, 2, 1024], P('section', None, 'fsdp')
- grad_bias_in: float32 [2, 4096], P('section', 'fsdp')
Inputs may be any that keep to these rules, and one draw needn't show every extreme that they name: `segment_ids`: within each aligned block of 64 rows the ids start at 0 and never fall; tokens of a block with equal ids form one sequence, of uneven length. In some block of every draw the ids reach 15.
All inputs are finite; a program needn't handle non-finite values.
Results may differ from a plain program's by a relative error of at most 0.013.
Values may be sent and summed in bfloat16 or wider, within the bound.
A program may use at most 320 MiB of HBM per device.

v0:
```python
import jax
import jax.numpy as jnp
from jax import lax
from jax.sharding import PartitionSpec as P

HEADS = 16
HEAD_DIM = 64
SEQ = 64
MICRO = 4


EPSILON = 1e-05


def from_behind(block, axis, distance):
    devices = range(lax.axis_size(axis))
    route = [(i - distance, i) for i in devices if i - distance in devices]
    return lax.ppermute(block, axis, route)


def norm_forward(summed, gain_row, offset):
    center = summed - jnp.mean(summed, axis=-1, keepdims=True)
    inverse = lax.rsqrt(jnp.mean(center * center, axis=-1, keepdims=True) + EPSILON)
    normed = center * inverse
    return (normed * gain_row + offset, normed, inverse)


def norm_backward(grad_rows, normed, inverse, gain_row):
    scaled = grad_rows * gain_row
    return inverse * (
        scaled
        - jnp.mean(scaled, axis=-1, keepdims=True)
        - normed * jnp.mean(scaled * normed, axis=-1, keepdims=True)
    )


def gelu_slope(pre_act):
    return (
        0.5 * (1.0 + lax.erf(pre_act * 0.7071067811865476))
        + pre_act * jnp.exp(-0.5 * pre_act * pre_act) * 0.3989422804014327
    )


def masked_scores(query_heads, key_heads, segment):
    scores = jnp.einsum(
        "qhd,khd->hqk", query_heads, key_heads, preferred_element_type=jnp.float32
    ) * HEAD_DIM ** (-0.5)
    same_block = segment[:, None] == segment[None, :]
    return jnp.where(same_block[None], scores, -1e30)


def split_heads(rows_low):
    return rows_low.reshape(rows_low.shape[0], HEADS, HEAD_DIM)


def attend(query_rows, key_rows, value_rows, segment):
    scores = masked_scores(split_heads(query_rows), split_heads(key_rows), segment)
    row_peak = jnp.max(scores, axis=-1, keepdims=True)
    exponent = jnp.exp(scores - row_peak)
    row_total = jnp.sum(exponent, axis=-1, keepdims=True)
    weights = (exponent / row_total).astype(jnp.bfloat16)
    log_total = row_peak + jnp.log(row_total)
    context = jnp.einsum(
        "hqk,khd->qhd", weights, split_heads(value_rows), preferred_element_type=jnp.float32
    )
    return (context.reshape(query_rows.shape).astype(jnp.bfloat16), log_total)


def attend_backward(query_rows, key_rows, value_rows, log_total, context_grad, segment):
    query_heads = split_heads(query_rows)
    key_heads = split_heads(key_rows)
    grad_heads = split_heads(context_grad)
    probabilities = jnp.exp(masked_scores(query_heads, key_heads, segment) - log_total)
    prob_low = probabilities.astype(jnp.bfloat16)
    value_grad = jnp.einsum(
        "hqk,qhd->khd", prob_low, grad_heads, preferred_element_type=jnp.float32
    )
    weight_grad = jnp.einsum(
        "qhd,khd->hqk", grad_heads, split_heads(value_rows), preferred_element_type=jnp.float32
    )
    row_inner = jnp.sum(probabilities * weight_grad, axis=-1, keepdims=True)
    score_low = (probabilities * (weight_grad - row_inner) * HEAD_DIM ** (-0.5)).astype(
        jnp.bfloat16
    )
    query_grad = jnp.einsum(
        "hqk,khd->qhd", score_low, key_heads, preferred_element_type=jnp.float32
    )
    key_grad = jnp.einsum(
        "hqk,qhd->khd", score_low, query_heads, preferred_element_type=jnp.float32
    )
    shape_out = query_rows.shape
    return (
        query_grad.reshape(shape_out),
        key_grad.reshape(shape_out),
        value_grad.reshape(shape_out),
    )


def layer_forward(params, rows_in, segment):
    w_qkv, w_out, w_in, w_down, biases, gains, bias_in = params
    model_width = w_out.shape[0]
    projected = jnp.dot(rows_in, w_qkv, preferred_element_type=jnp.float32)
    query_rows = (projected[:, :model_width] + biases[0]).astype(jnp.bfloat16)
    key_rows = projected[:, model_width : 2 * model_width].astype(jnp.bfloat16)
    value_rows = (projected[:, 2 * model_width :] + biases[1]).astype(jnp.bfloat16)
    context, log_total = attend(query_rows, key_rows, value_rows, segment)
    first_sum = (
        rows_in.astype(jnp.float32)
        + jnp.dot(context, w_out, preferred_element_type=jnp.float32)
        + biases[2]
    )
    normed_out, first_normed, first_inverse = norm_forward(first_sum, gains[0], biases[3])
    normed_low = normed_out.astype(jnp.bfloat16)
    pre_act = jnp.dot(normed_low, w_in, preferred_element_type=jnp.float32) + bias_in
    activated = jax.nn.gelu(pre_act, approximate=False).astype(jnp.bfloat16)
    second_sum = (
        normed_out + jnp.dot(activated, w_down, preferred_element_type=jnp.float32) + biases[4]
    )
    result, second_normed, second_inverse = norm_forward(second_sum, gains[1], biases[5])
    kept_values = (
        rows_in,
        query_rows,
        key_rows,
        value_rows,
        log_total,
        context,
        first_normed,
        first_inverse,
        normed_low,
        pre_act,
        activated,
        second_normed,
        second_inverse,
        segment,
    )
    return (result.astype(jnp.bfloat16), kept_values)


def layer_backward(params, kept_values, cotangent):
    w_qkv, w_out, w_in, w_down, biases, gains, bias_in = params
    (
        rows_in,
        query_rows,
        key_rows,
        value_rows,
        log_total,
        context,
        first_normed,
        first_inverse,
        normed_low,
        pre_act,
        activated,
        second_normed,
        second_inverse,
        segment,
    ) = kept_values
    second_grad = norm_backward(cotangent, second_normed, second_inverse, gains[1])
    second_low = second_grad.astype(jnp.bfloat16)
    act_grad = jnp.dot(second_low, w_down.T, preferred_element_type=jnp.float32)
    pre_grad = act_grad * gelu_slope(pre_act)
    pre_low = pre_grad.astype(jnp.bfloat16)
    normed_grad = second_grad + jnp.dot(pre_low, w_in.T, preferred_element_type=jnp.float32)
    first_grad = norm_backward(normed_grad, first_normed, first_inverse, gains[0])
    first_low = first_grad.astype(jnp.bfloat16)
    context_grad = jnp.dot(first_low, w_out.T, preferred_element_type=jnp.float32).astype(
        jnp.bfloat16
    )
    query_grad, key_grad, value_grad = attend_backward(
        query_rows, key_rows, value_rows, log_total, context_grad, segment
    )
    joined = jnp.concatenate([query_grad, key_grad, value_grad], axis=1).astype(jnp.bfloat16)
    input_grad = first_grad + jnp.dot(joined, w_qkv.T, preferred_element_type=jnp.float32)
    bias_grads = jnp.stack(
        [
            jnp.sum(query_grad, axis=0),
            jnp.sum(value_grad, axis=0),
            jnp.sum(first_grad, axis=0),
            jnp.sum(normed_grad, axis=0),
            jnp.sum(second_grad, axis=0),
            jnp.sum(cotangent, axis=0),
        ]
    )
    gain_grads = jnp.stack(
        [jnp.sum(normed_grad * first_normed, axis=0), jnp.sum(cotangent * second_normed, axis=0)]
    )
    low_parts = (joined, first_low, pre_low, second_low)
    return (input_grad, low_parts, (bias_grads, gain_grads, jnp.sum(pre_grad, axis=0)))


def body(ends_in, segment_ids, w_qkv, w_out, w_in, w_down, biases, gains, bias_in):
    section_index = lax.axis_index("section")
    sections = lax.axis_size("section")
    tick_count = MICRO + sections - 1
    local_rows = ends_in[0]
    model_width = local_rows.shape[1]
    shard_rows = w_out.shape[1]
    ff_width = w_in.shape[2]
    widen = ff_width // model_width
    shards = (w_qkv[0], w_out[0], w_in[0], w_down[0], biases[0], gains[0], bias_in[0])

    def fetch_layer():
        return (
            lax.all_gather(shards[0], "fsdp", axis=0, tiled=True),
            lax.all_gather(shards[1], "fsdp", axis=0, tiled=True),
            lax.all_gather(shards[2], "fsdp", axis=0, tiled=True),
            lax.all_gather(shards[3], "fsdp", axis=0, tiled=True),
            lax.all_gather(shards[4], "fsdp", axis=1, tiled=True),
            lax.all_gather(shards[5], "fsdp", axis=1, tiled=True),
            lax.all_gather(shards[6], "fsdp", axis=0, tiled=True),
        )

    params = fetch_layer()
    outputs_last = jnp.zeros_like(local_rows)
    carried = jnp.zeros((SEQ, model_width), jnp.bfloat16)
    kept_list = []
    for tick_index in range(tick_count):
        micro_index = tick_index - section_index
        is_valid = jnp.logical_and(micro_index >= 0, micro_index < MICRO)
        row_start = jnp.clip(micro_index, 0, MICRO - 1) * SEQ
        own_rows = lax.dynamic_slice_in_dim(local_rows, row_start, SEQ, 0)
        segment = lax.dynamic_slice_in_dim(segment_ids, row_start, SEQ, 0)
        entering = jnp.where(section_index == 0, own_rows, carried)
        result, kept_values = layer_forward(params, entering, segment)
        kept_list.append(kept_values)
        previous = lax.dynamic_slice_in_dim(outputs_last, row_start, SEQ, 0)
        outputs_last = lax.dynamic_update_slice_in_dim(
            outputs_last, jnp.where(is_valid, result, previous), row_start, 0
        )
        if tick_index + 1 < tick_count:
            carried = from_behind(result, "section", 1)
    stacked = jax.tree.map(lambda *leaves: jnp.stack(leaves), *kept_list)
    params = fetch_layer()
    inputs_grad = jnp.zeros_like(local_rows)
    carried = jnp.zeros((SEQ, model_width), jnp.bfloat16)
    small_totals = (
        jnp.zeros((6, model_width), jnp.float32),
        jnp.zeros((2, model_width), jnp.float32),
        jnp.zeros((ff_width,), jnp.float32),
    )
    low_list = []
    for tick_index in range(tick_count):
        micro_index = tick_index - (sections - 1 - section_index)
        is_valid = jnp.logical_and(micro_index >= 0, micro_index < MICRO)
        row_start = jnp.clip(micro_index, 0, MICRO - 1) * SEQ
        own_rows = lax.dynamic_slice_in_dim(local_rows, row_start, SEQ, 0)
        cotangent = jnp.where(section_index == sections - 1, own_rows, carried).astype(jnp.float32)
        cotangent = cotangent * is_valid.astype(jnp.float32)
        forward_tick = jnp.clip(micro_index + section_index, 0, tick_count - 1)
        kept_values = jax.tree.map(
            lambda member: lax.dynamic_index_in_dim(member, forward_tick, 0, keepdims=False),
            stacked,
        )
        backward, low_parts, small_sums = layer_backward(params, kept_values, cotangent)
        low_list.append(low_parts)
        small_totals = tuple(
            (running + increment for running, increment in zip(small_totals, small_sums))
        )
        backward_low = backward.astype(jnp.bfloat16)
        previous = lax.dynamic_slice_in_dim(inputs_grad, row_start, SEQ, 0)
        inputs_grad = lax.dynamic_update_slice_in_dim(
            inputs_grad, jnp.where(is_valid, backward_low, previous), row_start, 0
        )
        if tick_index + 1 < tick_count:
            carried = from_behind(backward_low, "section", -1)
    low_stack = jax.tree.map(lambda *leaves: jnp.stack(leaves), *low_list)

    def valid_rows(member, first_tick):
        chosen = lax.dynamic_slice_in_dim(member, first_tick, MICRO, 0)
        return chosen.reshape((MICRO * chosen.shape[1],) + chosen.shape[2:])

    backward_first = sections - 1 - section_index
    inputs_all = valid_rows(stacked[0], section_index)
    context_all = valid_rows(stacked[5], section_index)
    normed_all = valid_rows(stacked[8], section_index)
    activated_all = valid_rows(stacked[10], section_index)
    joined_all = valid_rows(low_stack[0], backward_first)
    first_all = valid_rows(low_stack[1], backward_first)
    pre_all = valid_rows(low_stack[2], backward_first)
    second_all = valid_rows(low_stack[3], backward_first)
    part_qkv = jnp.einsum("ta,tb->ab", inputs_all, joined_all, preferred_element_type=jnp.float32)
    part_out = jnp.einsum("ta,tb->ab", context_all, first_all, preferred_element_type=jnp.float32)
    part_in = jnp.einsum("ta,tb->ab", normed_all, pre_all, preferred_element_type=jnp.float32)
    part_down = jnp.einsum(
        "ta,tb->ab", activated_all, second_all, preferred_element_type=jnp.float32
    ).reshape(shard_rows * lax.axis_size("fsdp"), widen * model_width)
    combined = lax.psum_scatter(
        jnp.concatenate([part_qkv, part_out, part_in, part_down], axis=1),
        "fsdp",
        scatter_dimension=0,
        tiled=True,
    )
    small_parts = (
        lax.psum_scatter(small_totals[0], "fsdp", scatter_dimension=1, tiled=True),
        lax.psum_scatter(small_totals[1], "fsdp", scatter_dimension=1, tiled=True),
        lax.psum_scatter(small_totals[2], "fsdp", scatter_dimension=0, tiled=True),
    )
    totals = lax.psum((combined, small_parts[0], small_parts[1], small_parts[2]), "replica")
    combined_total, bias_part, gain_part, bias_in_part = totals
    grad_qkv_part = combined_total[:, : 3 * model_width]
    grad_out_part = combined_total[:, 3 * model_width : 4 * model_width]
    grad_in_part = combined_total[:, 4 * model_width : 4 * model_width + ff_width]
    grad_down_part = combined_total[:, 4 * model_width + ff_width :].reshape(
        shard_rows * widen, model_width
    )
    ends_out = jnp.where(section_index == 0, inputs_grad, outputs_last)[None]
    return (
        ends_out,
        grad_qkv_part[None],
        grad_out_part[None],
        grad_in_part[None],
        grad_down_part[None],
        bias_part[None],
        gain_part[None],
        bias_in_part[None],
    )


def solution(mesh):
    in_specs = (
        P("section", ("fsdp", "replica"), None),
        P(("fsdp", "replica")),
        P("section", "fsdp", None),
        P("section", "fsdp", None),
        P("section", "fsdp", None),
        P("section", "fsdp", None),
        P("section", None, "fsdp"),
        P("section", None, "fsdp"),
        P("section", "fsdp"),
    )
    out_specs = (
        P("section", ("fsdp", "replica"), None),
        P("section", "fsdp", None),
        P("section", "fsdp", None),
        P("section", "fsdp", None),
        P("section", "fsdp", None),
        P("section", None, "fsdp"),
        P("section", None, "fsdp"),
        P("section", "fsdp"),
    )
    return jax.shard_map(body, mesh=mesh, in_specs=in_specs, out_specs=out_specs, check_vma=False)
```

profile of v0, /device:TPU:6, one launch (start us, length us, event | category | flops | bytes accessed | tf_op | source)
XLA Modules:
  0.0 1313.8 jit_solution(15540144495663350739)
XLA Ops:
  10.1 12.1 all-gather.5
  22.4 9.6 all-gather.3
  32.0 11.2 all-gather.1
  47.5 5.6 all-gather.12.cloned.1.call-done
  60.0 20.0 %all-gather.14.cloned.1.call-done = bf16[1,1024,1024]{2,1,0:T(8,128)(2,1)} async-done(((bf16[1,128,1024]{2,1,0:T(8,128)(2,1)}), bf16[1,1024,1024]{2,1,0:T(8,128)(2,1)}) %all-gather.14.cloned.1.call-update) | async-done | bytes 2097168 | tf_op jit(solution)/shard_map/all_gather | solution.py:204
  85.2 46.6 %all-gather.16.cloned.1.call-done = bf16[1,1024,4096]{2,1,0:T(8,128)(2,1)} async-done(((bf16[1,128,4096]{2,1,0:T(8,128)(2,1)}), bf16[1,1024,4096]{2,1,0:T(8,128)(2,1)}) %all-gather.16.cloned.1.call-update) | async-done | bytes 8388624 | tf_op jit(solution)/shard_map/all_gather | solution.py:205
  131.8 8.2 bitcast_dynamic-update-slice_fusion.9
  140.0 43.3 %all-gather.18.cloned.1.call-done = bf16[1,4096,1024]{2,1,0:T(8,128)(2,1)} async-done(((bf16[1,512,1024]{2,1,0:T(8,128)(2,1)}), bf16[1,4096,1024]{2,1,0:T(8,128)(2,1)}) %all-gather.18.cloned.1.call-update) | async-done | bytes 8388624 | tf_op jit(solution)/shard_map/all_gather | solution.py:206
  211.8 8.0 bitcast_dynamic-update-slice_fusion.8
  250.3 8.1 bitcast_dynamic-update-slice_fusion.7
  287.7 8.0 bitcast_dynamic-update-slice_fusion.6
  336.1 8.0 bitcast_dynamic-update-slice_fusion.5
  344.2 5.3 fusion.673
  409.7 5.7 select_dynamic-update-slice_fusion.7
  436.1 7.2 bitcast_dynamic-update-slice_fusion.13
  443.3 7.1 fusion.437
  478.9 5.8 select_dynamic-update-slice_fusion.6
  495.4 7.3 bitcast_dynamic-update-slice_fusion.12
  536.4 5.8 select_dynamic-update-slice_fusion.5
  552.3 7.3 bitcast_dynamic-update-slice_fusion.11
  593.2 5.8 select_dynamic-update-slice_fusion.4
  609.2 7.3 bitcast_dynamic-update-slice_fusion.10
  633.6 9.7 convolution_bitcast_fusion
  643.3 20.6 %reshape.1429 = f32[1024,4096]{1,0:T(8,128)} reshape(f32[4096,1024]{1,0:T(8,128)} %convolution_bitcast_fusion) | data formatting | bytes 33554432 | tf_op jit(solution)/shard_map/reshape | solution.py:285
  667.9 6.3 convolution_bitcast_fusion.2
  674.2 8.2 convolution_bitcast_fusion.1
  682.4 33.2 %pad_maximum_fusion = f32[1024,12288]{1,0:T(8,128)} fusion(f32[1024,4096]{1,0:T(8,128)} %reshape.1429, f32[1024,4096]{1,0:T(8,128)} %convolution_bitcast_fusion.1, f32[1024,1024]{1,0:T(8,128)} %convolution_bitcast_fusion.3, f32[1024,3072]{1,0:T(8,128)} %convolution_bitcast_fusion.2), kind=kLoop, calls=%fused_computation.5 | loop fusion | flops 37748736 | bytes 100663296 | tf_op jit(solution)/shard_map/concatenate | solution.py:287
  720.1 245.2 %reduce-scatter.6.cloned.1.call-done = f32[128,12288]{1,0:T(8,128)} async-done(((f32[1024,12288]{1,0:T(8,128)}), f32[128,12288]{1,0:T(8,128)}) %reduce-scatter.6.cloned.1.call-update) | async-done | bytes 6291472 | tf_op jit(solution)/shard_map/reduce_scatter | solution.py:286
  972.0 23.7 %all-reduce = f32[4096]{0:T(1024)S(1)} all-reduce(f32[4096]{0:T(1024)S(1)} %add_add_fusion.5), channel_id=12, replica_groups=mesh['section'=2,'fsdp'=8,'replica'=8] {'fsdp'}, use_global_device_ids=true, to_apply=%region_106.107.clone | all-reduce | flops 4096 | bytes 32768
  1002.4 28.4 %reduce-scatter.8.cloned.1.call-done = f32[6,128]{1,0:T(8,128)} async-done(((f32[6,1024]{1,0:T(8,128)}), f32[6,128]{1,0:T(8,128)}) %reduce-scatter.8.cloned.1.call-update) | async-done | bytes 3088 | tf_op jit(solution)/shard_map/reduce_scatter | solution.py:293
  1031.5 25.4 %all-reduce.1 = (f32[1,6,128]{2,0,1:T(1,128)}, f32[1,2,128]{2,1,0:T(2,128)}, f32[1,512]{1,0:T(1,128)}) all-reduce(f32[1,6,128]{2,0,1:T(1,128)S(1)} %broadcast_in_dim.110, f32[1,2,128]{2,1,0:T(2,128)S(1)} %bitcast.990, f32[1,512]{1,0:T(1,128)S(1)} %bitcast.984), channel_id=1, replica_groups=mesh['section'=2,'fsdp'=8,'replica'=8] {'replica'}, use_global_device_ids=true, to_apply=%region_88.89 | all-reduce | flops 1536 | bytes 12288 | tf_op jit(solution)/shard_map/psum | solution.py:297
  1056.9 239.5 %all-reduce.4.cloned.1.call-done = f32[128,12288]{1,0:T(8,128)} async-done(((f32[128,12288]{1,0:T(8,128)}), f32[128,12288]{1,0:T(8,128)}) %all-reduce.4.cloned.1.call-update) | async-done | bytes 6291472 | tf_op jit(solution)/shard_map/psum | solution.py:297
  (749 shorter events, 402.7 us)
Async XLA Ops:
  7.2 15.1 %copy-start.141 = (s32[256]{0:T(256)S(1)}, s32[256]{0:T(256)}, u32[]{:S(2)}) copy-start(s32[256]{0:T(256)} %param.10) | copy-start | bytes 3076
  7.2 15.2 %copy-start.166 = (bf16[1,2,128]{2,1,0:T(2,128)(2,1)S(1)}, bf16[1,2,128]{2,1,0:T(2,128)(2,1)}, u32[]{:S(2)}) copy-start(bf16[1,2,128]{2,1,0:T(2,128)(2,1)} %param.16) | copy-start | bytes 1540
  7.2 24.8 %copy-start.163 = (bf16[1,6,128]{2,1,0:T(8,128)(2,1)S(1)}, bf16[1,6,128]{2,1,0:T(8,128)(2,1)}, u32[]{:S(2)}) copy-start(bf16[1,6,128]{2,1,0:T(8,128)(2,1)} %param.15) | copy-start | bytes 4612
  7.2 36.1 %copy-start.10 = (bf16[1,256,1024]{2,1,0:T(8,128)(2,1)S(1)}, bf16[1,256,1024]{2,1,0:T(8,128)(2,1)}, u32[]{:S(2)}) copy-start(bf16[1,256,1024]{2,1,0:T(8,128)(2,1)} %param.9) | copy-start | bytes 1572868
  7.2 45.9 %all-gather.12.cloned.1.call-start = ((), (), s32[]{:S(2)}) async-start(), calls=%async_computation.6 | async-start | bytes 7077888 | tf_op jit(solution)/shard_map/all_gather | solution.py:203
  8.0 72.0 %all-gather.14.cloned.1.call-start = ((), (), s32[]{:S(2)}) async-start(), calls=%async_computation.7 | async-start | bytes 2359296 | tf_op jit(solution)/shard_map/all_gather | solution.py:204
  8.7 123.1 %all-gather.16.cloned.1.call-start = ((), (), s32[]{:S(2)}) async-start(), calls=%async_computation.8 | async-start | bytes 9437184 | tf_op jit(solution)/shard_map/all_gather | solution.py:205
  9.4 173.8 %all-gather.18.cloned.1.call-start = ((), (), s32[]{:S(2)}) async-start(), calls=%async_computation.9 | async-start | bytes 9437184 | tf_op jit(solution)/shard_map/all_gather | solution.py:206
  10.0 955.3 %reduce-scatter.6.cloned.1.call-start = ((), (), s32[]{:S(2)}) async-start(), calls=%async_computation.3 | async-start | bytes 56623104 | tf_op jit(solution)/shard_map/reduce_scatter | solution.py:286
  22.2 109.5 %copy-start.124 = (f32[1,4096]{1,0:T(1,128)}, f32[1,4096]{1,0:T(1,128)S(1)}, u32[]{:S(2)}) copy-start(f32[1,4096]{1,0:T(1,128)S(1)} %convert_element_type.557) | copy-start | bytes 49156
  47.5 135.8 %copy-start.79 = (f32[1,1,1024]{2,1,0:T(1,128)}, f32[1,1,1024]{2,1,0:T(1,128)S(1)}, u32[]{:S(2)}) copy-start(f32[1,1,1024]{2,1,0:T(1,128)S(1)} %get-tuple-element.201) | copy-start | bytes 12292
  47.5 142.2 %copy-start.74 = (f32[1,1,1024]{2,1,0:T(1,128)}, f32[1,1,1024]{2,1,0:T(1,128)S(1)}, u32[]{:S(2)}) copy-start(f32[1,1,1024]{2,1,0:T(1,128)S(1)} %get-tuple-element.200) | copy-start | bytes 12292
  190.5 6.6 collective-permute-start
  223.6 8.6 collective-permute-start.1
  262.2 7.2 collective-permute-start.2
  299.5 7.4 collective-permute-start.3
  375.8 21.4 %copy-start.14 = (f32[64,1024]{1,0:T(8,128)S(1)}, f32[64,1024]{1,0:T(8,128)}, u32[]{:S(2)}) copy-start(f32[64,1024]{1,0:T(8,128)} %copy-done.12) | copy-start | bytes 786436
  415.5 17.2 %collective-permute-start.4 = (bf16[64,1024]{1,0:T(8,128)(2,1)}, bf16[64,1024]{1,0:T(8,128)(2,1)}, u32[]{:S(2)}, u32[]{:S(2)}) collective-permute-start(bf16[64,1024]{1,0:T(8,128)(2,1)} %get-tuple-element.259), channel_id=1, source_target_pairs={{64,0},{65,1},{66,2},{67,3},{68,4},{69,5},{70,6},{71,7},{72,8},{73... | collective-permute-start | bytes 393224 | tf_op jit(solution)/shard_map/ppermute | solution.py:18
  478.9 14.9 %copy-start.158 = (f32[64]{0:T(128)S(1)}, f32[64]{0:T(128)}, u32[]{:S(2)}) copy-start(f32[64]{0:T(128)} %get-tuple-element.220) | copy-start | bytes 772
  478.9 23.8 %slice-start.12 = ((s8[8388608]{0:T(1024)(128)(4,1)}), s8[4194304]{0:T(1024)(128)(4,1)S(1)}, s32[]{:S(2)}) async-start(s8[8388608]{0:T(1024)(128)(4,1)} %bitcast.825), calls=%async_computation.23 | async-start | bytes 8388608
  484.6 7.4 collective-permute-start.5
  536.3 23.3 %slice-start.14 = ((s8[8388608]{0:T(1024)(128)(4,1)}), s8[4194304]{0:T(1024)(128)(4,1)S(1)}, s32[]{:S(2)}) async-start(s8[8388608]{0:T(1024)(128)(4,1)} %bitcast.827), calls=%async_computation.25 | async-start | bytes 8388608
  542.1 6.8 collective-permute-start.6
  593.2 23.2 %slice-start.16 = ((s8[8388608]{0:T(1024)(128)(4,1)}), s8[4194304]{0:T(1024)(128)(4,1)S(1)}, s32[]{:S(2)}) async-start(s8[8388608]{0:T(1024)(128)(4,1)} %bitcast.829), calls=%async_computation.27 | async-start | bytes 8388608
  599.0 6.8 collective-permute-start.7
  627.1 16.2 %copy-start.36 = (bf16[16,64,64]{2,1,0:T(8,128)(2,1)}, bf16[16,64,64]{2,1,0:T(8,128)(2,1)S(1)}, u32[]{:S(2)}) copy-start(bf16[16,64,64]{2,1,0:T(8,128)(2,1)S(1)} %convolution_convert_fusion) | copy-start | bytes 393220
  643.3 20.6 %copy-start.91 = (bf16[5,64,1024]{2,1,0:T(8,128)(2,1)S(1)}, bf16[5,64,1024]{2,1,0:T(8,128)(2,1)}, u32[]{:S(2)}) copy-start(bf16[5,64,1024]{2,1,0:T(8,128)(2,1)} %constant_dynamic-update-slice_fusion.40) | copy-start | bytes 1966084
  716.0 285.5 %reduce-scatter.10.cloned.1.call-start = ((), (), s32[]{:S(2)}) async-start(), calls=%async_computation.10 | async-start | bytes 589824
  719.3 311.5 %reduce-scatter.8.cloned.1.call-start = ((), (), s32[]{:S(2)}) async-start(), calls=%async_computation.5 | async-start | bytes 36864 | tf_op jit(solution)/shard_map/reduce_scatter | solution.py:293
  720.1 576.3 %all-reduce.4.cloned.1.call-start = ((), (), s32[]{:S(2)}) async-start(), calls=%async_computation.4 | async-start | bytes 12582912 | tf_op jit(solution)/shard_map/psum | solution.py:297
  969.1 26.7 %copy-start.24 = (f32[64,1024]{1,0:T(8,128)S(1)}, f32[64,1024]{1,0:T(8,128)}, u32[]{:S(2)}) copy-start(f32[64,1024]{1,0:T(8,128)} %copy-done.22) | copy-start | bytes 786436
  969.3 26.5 %copy-start.16 = (bf16[256,1024]{1,0:T(8,128)(2,1)S(1)}, bf16[256,1024]{1,0:T(8,128)(2,1)}, u32[]{:S(2)}) copy-start(bf16[256,1024]{1,0:T(8,128)(2,1)} %get-tuple-element.273) | copy-start | bytes 1572868
  (170 other events, 904.9 us)
Sparse Core Ops, SparseCore 0:
  9.7 43.3 all-gather.11
  54.9 25.0 all-gather.13
  81.7 50.0 all-gather.15
  133.3 49.8 all-gather.17
  716.1 249.1 reduce-scatter.5
  968.2 30.5 reduce-scatter.9
  1001.8 29.0 reduce-scatter.7
  1033.5 262.7 all-reduce.3
where the time goes:
time: 1330 us; the launch traced here: 1310 us
  waiting for transfers between devices  645 us (48%)
  matrix products  261 us (20%)
  local copies, waits for them, and re-layouts  168 us (13%)
  other arithmetic  116 us (9%)
  blocking collectives  82.1 us (6%)
  starting transfers between devices  23.4 us (2%)
  between operations  17.7 us (1%)
    reduce_scatter x1, waiting for transfers between devices, body(): lax.psum_scatter(jnp.concatenate([part_qkv, part_out, part_in, part_down]...  245 us
    psum x1, waiting for transfers between devices, body(): lax.psum((combined, small_parts[0], small_parts[1], small_parts[2]), 'rep...  239 us
    reshape x35, local copies, waits for them, and re-layouts, split_heads(): return rows_low.reshape(rows_low.shape[0], HEADS, HEAD_DIM)  49.5 us
    all_gather x1, waiting for transfers between devices, fetch_layer(): lax.all_gather(shards[2], 'fsdp', axis=0, tiled=True)  46.6 us
    all_gather x1, waiting for transfers between devices, fetch_layer(): lax.all_gather(shards[3], 'fsdp', axis=0, tiled=True)  43.3 us
    dot_general x5, matrix products, layer_forward(): jnp.dot(normed_low, w_in, preferred_element_type=jnp.float32) + bias_in  40.4 us
    unnamed x53, other arithmetic  34.8 us
    dot_general x5, matrix products, layer_backward(): act_grad = jnp.dot(second_low, w_down.T, preferred_element_type=jnp.float32)  33.9 us
  transfers between devices with their start and end apart: 16, of which 11 were waited for; matrix products, arithmetic and copies ran while one was open for 5% of the time, Pallas kernels for 0%

commit v1 on v0

v1 whole, which is shorter than its diff:
```python
import jax
import jax.numpy as jnp
from jax import lax
from jax.experimental import pallas as pl
from jax.experimental.pallas import tpu as pltpu
from jax.sharding import PartitionSpec as P

HEADS = 16
HEAD_DIM = 64
SEQ = 64
MICRO = 4


EPSILON = 1e-05


MESH = pl.DeviceIdType.MESH
N_F = 8
TILE = 128
SMALL_ROWS = 16
PAYLOAD = 97 * TILE
VMEM_CAP = 60 * 1024 * 1024

GATHER_PLAN = ((128, 3072, 16), (128, 1024, 16), (128, 4096, 16), (512, 1024, 128), (16, 256, 0))


def place():
    f = lax.axis_index("fsdp")
    r = lax.axis_index("replica")
    return f // 2, lax.rem(f, 2), r // 2, lax.rem(r, 2)


def device(y, c, x, z):
    return {"fsdp": y * 2 + c, "replica": x * 2 + z}


def step_on(index, distance):
    return lax.rem(index + distance + 4, 4)


def greet(peers):
    barrier = pltpu.get_barrier_semaphore()
    for peer in peers:
        pl.semaphore_signal(barrier, inc=1, device_id=peer, device_id_type=MESH)
    pl.semaphore_wait(barrier, len(peers))


class Copies:
    def __init__(self, send_sem, recv_sem):
        self.send_sem, self.recv_sem, self.started = send_sem, recv_sem, []

    def start(self, src, dst, peer):
        number = len(self.started)
        copy = pltpu.make_async_remote_copy(
            src_ref=src,
            dst_ref=dst,
            send_sem=self.send_sem.at[number],
            recv_sem=self.recv_sem.at[number],
            device_id=peer,
            device_id_type=MESH,
        )
        copy.start()
        self.started.append(copy)
        return copy

    def finish(self):
        for copy in self.started:
            copy.wait_send()


def gather_kernel(*refs):
    count = len(GATHER_PLAN)
    ins, outs = refs[:count], refs[count : 2 * count]
    send_sem, recv_sem, local_sem = refs[2 * count :]
    y, c, x, z = place()
    right_y, left_y = device(step_on(y, 1), c, x, z), device(step_on(y, -1), c, x, z)
    right_x, left_x = device(y, c, step_on(x, 1), z), device(y, c, step_on(x, -1), z)
    sibling = device(y, 1 - c, x, z)
    greet((right_y, left_y, right_x, left_x, sibling))
    copies = Copies(send_sem, recv_sem)

    def span(k, owner_y, first, rows, part=None):
        shard_rows, columns, _ = GATHER_PLAN[k]
        start = pl.multiple_of((owner_y * 2 + c) * shard_rows + first, 16)
        if part is None:
            return outs[k].at[pl.ds(start, rows), :]
        half = columns // 2
        return outs[k].at[pl.ds(start, rows), pl.ds(part * half, half)]

    def quarter(k, owner_x):
        return pl.multiple_of(owner_x * GATHER_PLAN[k][2], 16)

    relayed = [k for k in range(count) if GATHER_PLAN[k][2]]
    direct = [k for k in range(count) if GATHER_PLAN[k][0] > 4 * GATHER_PLAN[k][2]]
    first_right, first_left = {}, {}
    for kind, members in (("relay", relayed), ("direct", direct)):
        for k in members:
            shard_rows, _, piece = GATHER_PLAN[k]
            if kind == "relay":
                first, rows = quarter(k, x), piece
            else:
                first, rows = 4 * piece, shard_rows - 4 * piece
            src = ins[k].at[pl.ds(first, rows), :]
            first_right[kind, k] = copies.start(src, span(k, y, first, rows), right_y)
            first_left[kind, k] = copies.start(src, span(k, y, first, rows), left_y)
    own = []
    sibling_copies = []
    for k in range(count):
        shard_rows = GATHER_PLAN[k][0]
        own.append(pltpu.make_async_copy(ins[k], span(k, y, 0, shard_rows), local_sem.at[k]))
        own[-1].start()
        sibling_copies.append(copies.start(ins[k], span(k, y, 0, shard_rows), sibling))

    before, after, across = step_on(y, -1), step_on(y, 1), step_on(y, 2)
    second_right, second_left = {}, {}
    along_right, along_left = {}, {}
    for kind, members in (("relay", relayed), ("direct", direct)):
        for k in members:
            shard_rows, _, piece = GATHER_PLAN[k]
            if kind == "relay":
                first, rows = quarter(k, x), piece
            else:
                first, rows = 4 * piece, shard_rows - 4 * piece
            first_right[kind, k].wait_recv()
            block = span(k, before, first, rows, 0)
            second_right[kind, k] = copies.start(block, block, right_y)
            first_left[kind, k].wait_recv()
            block = span(k, after, first, rows, 1)
            second_left[kind, k] = copies.start(block, block, left_y)
            if kind == "relay":
                for n, owner in ((0, before), (1, after)):
                    block = span(k, owner, first, rows)
                    along_right[n, k] = copies.start(block, block, right_x)
                    along_left[n, k] = copies.start(block, block, left_x)
    for k in relayed:
        second_right["relay", k].wait_recv()
        second_left["relay", k].wait_recv()
        block = span(k, across, quarter(k, x), GATHER_PLAN[k][2])
        along_right[2, k] = copies.start(block, block, right_x)
        along_left[2, k] = copies.start(block, block, left_x)
    further = {}
    owners = (before, after, across)
    for n in range(3):
        for k in relayed:
            piece = GATHER_PLAN[k][2]
            along_right[n, k].wait_recv()
            block = span(k, owners[n], quarter(k, step_on(x, -1)), piece, 0)
            further[n, k, 0] = copies.start(block, block, right_x)
            along_left[n, k].wait_recv()
            block = span(k, owners[n], quarter(k, step_on(x, 1)), piece, 1)
            further[n, k, 1] = copies.start(block, block, left_x)
    for n in range(3):
        for k in range(count):
            shard_rows = GATHER_PLAN[k][0]
            if n == 2 and k in direct:
                second_right["direct", k].wait_recv()
                second_left["direct", k].wait_recv()
            if k in relayed:
                further[n, k, 0].wait_recv()
                further[n, k, 1].wait_recv()
            block = span(k, owners[n], 0, shard_rows)
            sibling_copies.append(copies.start(block, block, sibling))
    for copy in own:
        copy.wait()
    for copy in sibling_copies:
        copy.wait_recv()
    copies.finish()


def gather_weights(*shards):
    copies = 160
    return pl.pallas_call(
        gather_kernel,
        out_shape=[
            jax.ShapeDtypeStruct((N_F * rows, columns), jnp.bfloat16)
            for rows, columns, _ in GATHER_PLAN
        ],
        in_specs=[pl.BlockSpec(memory_space=pl.ANY)] * len(GATHER_PLAN),
        out_specs=[pl.BlockSpec(memory_space=pl.ANY)] * len(GATHER_PLAN),
        scratch_shapes=[
            pltpu.SemaphoreType.DMA((copies,)),
            pltpu.SemaphoreType.DMA((copies,)),
            pltpu.SemaphoreType.DMA((len(GATHER_PLAN),)),
        ],
        compiler_params=pltpu.CompilerParams(
            collective_id=0, has_side_effects=True, vmem_limit_bytes=4 * 1024 * 1024
        ),
        name="gather_weights",
    )(*shards)


REDUCE_PLAN = ((8, 8, "y"), (8, 8, "x"), (8, 8, "y"), (8, 8, "y"), (8, 8, "x"), (8, 9, "y"))


def stage_shape(plan, stage):
    part_a, part_b, leading = plan
    rows = {("y", 0): (1, 128), ("x", 0): (4, 32), ("y", 1): (1, 32), ("x", 1): (1, 32)}
    blocks, height = rows[leading, stage]
    return blocks, height, (part_a + part_b) * TILE


def add_into(target, rows, columns, sources, dest=None):
    blocks, first_block, height, first_row = rows
    first_column, width = columns

    def one(step, carry):
        block, row = step // (height // 16), lax.rem(step, height // 16) * 16
        here = (
            first_block + block,
            pl.ds(pl.multiple_of(first_row + row, 16), 16),
            pl.ds(first_column, width),
        )
        total = target[here].astype(jnp.float32)
        for ref, base, column in sources:
            total = total + ref[
                base + block, pl.ds(pl.multiple_of(row, 16), 16), pl.ds(column, width)
            ].astype(jnp.float32)
        if dest is None:
            target[here] = total.astype(jnp.bfloat16)
        else:
            dest[pl.ds(pl.multiple_of(row, 16), 16), pl.ds(first_column, width)] = total.astype(
                jnp.bfloat16
            )
        return carry

    lax.fori_loop(0, blocks * (height // 16), one, 0)


def reduce_kernel(parts, out, held, paired, final, crossed, *rest):
    stage_refs, (send_sem, recv_sem, local_sem) = rest[:-3], rest[-3:]
    y, c, x, z = place()
    ring = {
        "y": (y, device(step_on(y, 1), c, x, z), device(step_on(y, -1), c, x, z)),
        "x": (x, device(y, c, step_on(x, 1), z), device(y, c, step_on(x, -1), z)),
    }
    sibling = device(y, 1 - c, x, z)
    partner = device(y, c, x, 1 - z)
    greet((ring["y"][1], ring["y"][2], ring["x"][1], ring["x"][2], sibling, partner))
    copies = Copies(send_sem, recv_sem)
    own, from_sibling, from_here, offset = [], [], [], 0
    offsets = []
    for n, (part_a, part_b, _) in enumerate(REDUCE_PLAN):
        width = (part_a + part_b) * TILE
        columns = pl.ds(offset, width)
        from_sibling.append(
            copies.start(parts.at[:, 1 - c, :, columns], paired.at[:, :, columns], sibling)
        )
        local = pltpu.make_async_copy(
            parts.at[:, c, :, columns], held.at[:, :, columns], local_sem.at[n]
        )
        local.start()
        from_here.append(local)
        offsets.append(offset)
        offset += width

    def along(n, stage):
        part_a, part_b, leading = REDUCE_PLAN[n]
        wide_a, wide_b = part_a * TILE, part_b * TILE
        start_a, start_b = offsets[n], offsets[n] + wide_a
        axis = leading if stage == 0 else ("x" if leading == "y" else "y")
        index, right, left = ring[axis]
        blocks, height, _ = stage_shape(REDUCE_PLAN[n], stage)
        landing = stage_refs[2 * n + stage]

        def origin(at):
            if axis == "y":
                return at, (0 if stage == 0 else x * 32)
            return (0 if stage == 0 else y), at * 32

        def take(at, start, wide):
            block, row = origin(at)
            return held.at[
                pl.ds(block, blocks), pl.ds(pl.multiple_of(row, 16), height), pl.ds(start, wide)
            ]

        def land(slot, start, wide):
            return landing.at[pl.ds(slot * blocks, blocks), :, pl.ds(start - offsets[n], wide)]

        def add(at, start, wide, slots):
            block, row = origin(at)
            add_into(
                held,
                (blocks, block, height, row),
                (start, wide),
                [(landing, slot * blocks, start - offsets[n]) for slot in slots],
            )

        ahead, behind, across = step_on(index, 1), step_on(index, -1), step_on(index, 2)
        far_right = copies.start(take(across, start_a, wide_a), land(0, start_a, wide_a), right)
        far_left = copies.start(take(across, start_b, wide_b), land(0, start_b, wide_b), left)
        near = [
            copies.start(take(ahead, start_b, wide_b), land(1, start_b, wide_b), right),
            copies.start(take(behind, start_a, wide_a), land(2, start_a, wide_a), left),
        ]
        yield
        far_right.wait_recv()
        add(ahead, start_a, wide_a, (0,))
        near.append(copies.start(take(ahead, start_a, wide_a), land(1, start_a, wide_a), right))
        far_left.wait_recv()
        add(behind, start_b, wide_b, (0,))
        near.append(copies.start(take(behind, start_b, wide_b), land(2, start_b, wide_b), left))
        yield
        for copy in near:
            copy.wait_recv()
        add(index, start_a, wide_a + wide_b, (1, 2))

    def chunk(n):
        part_a, part_b, _ = REDUCE_PLAN[n]
        start, wide_a, wide = offsets[n], part_a * TILE, (part_a + part_b) * TILE
        columns = pl.ds(start, wide)
        from_here[n].wait()
        from_sibling[n].wait_recv()
        add_into(held, (4, 0, 128, 0), (start, wide), [(paired, 0, start)])
        yield from along(n, 0)
        yield from along(n, 1)
        rows = pl.ds(pl.multiple_of(x * 32, 16), 32)
        swap = copies.start(held.at[pl.ds(y, 1), rows, columns], crossed.at[:, :, columns], partner)
        yield
        swap.wait_recv()
        add_into(held, (1, y, 32, x * 32), (start, wide), [(crossed, 0, start)], dest=final)
        kept = pltpu.make_async_copy(
            final.at[:, columns], out.at[rows, columns], local_sem.at[len(REDUCE_PLAN) + n]
        )
        kept.start()
        own.append(kept)
        _, right, left = ring["x"]
        to_right = copies.start(final.at[:, columns], out.at[rows, columns], right)
        to_left = copies.start(final.at[:, columns], out.at[rows, columns], left)
        yield
        to_right.wait_recv()
        block = out.at[
            pl.ds(pl.multiple_of(step_on(x, -1) * 32, 16), 32), pl.ds(start, wide_a)
        ]
        last = [copies.start(block, block, right)]
        to_left.wait_recv()
        block = out.at[
            pl.ds(pl.multiple_of(step_on(x, 1) * 32, 16), 32), pl.ds(start + wide_a, wide - wide_a)
        ]
        last.append(copies.start(block, block, left))
        yield
        for copy in last:
            copy.wait_recv()

    waiting = [chunk(n) for n in range(len(REDUCE_PLAN))]
    running = []
    while waiting or running:
        if waiting:
            running.append(waiting.pop(0))
        for member in list(running):
            if next(member, "end") == "end":
                running.remove(member)
    for copy in own:
        copy.wait()
    copies.finish()


def reduce_parts(parts):
    chunks = len(REDUCE_PLAN)
    landing = []
    for plan in REDUCE_PLAN:
        for stage in (0, 1):
            blocks, height, width = stage_shape(plan, stage)
            landing.append(pltpu.VMEM((3 * blocks, height, width), jnp.bfloat16))
    return pl.pallas_call(
        reduce_kernel,
        out_shape=jax.ShapeDtypeStruct((128, PAYLOAD), jnp.bfloat16),
        in_specs=[pl.BlockSpec(memory_space=pl.ANY)],
        out_specs=pl.BlockSpec(memory_space=pl.ANY),
        scratch_shapes=[
            pltpu.VMEM((4, 128, PAYLOAD), jnp.bfloat16),
            pltpu.VMEM((4, 128, PAYLOAD), jnp.bfloat16),
            pltpu.VMEM((32, PAYLOAD), jnp.bfloat16),
            pltpu.VMEM((1, 32, PAYLOAD), jnp.bfloat16),
            *landing,
            pltpu.SemaphoreType.DMA((chunks * 18,)),
            pltpu.SemaphoreType.DMA((chunks * 18,)),
            pltpu.SemaphoreType.DMA((chunks * 2,)),
        ],
        compiler_params=pltpu.CompilerParams(
            collective_id=1, has_side_effects=True, vmem_limit_bytes=VMEM_CAP
        ),
        name="reduce_parts",
    )(parts)


def norm_forward(summed, gain_row, offset):
    center = summed - jnp.mean(summed, axis=-1, keepdims=True)
    inverse = lax.rsqrt(jnp.mean(center * center, axis=-1, keepdims=True) + EPSILON)
    normed = center * inverse
    return (normed * gain_row + offset, normed, inverse)


def norm_backward(grad_rows, normed, inverse, gain_row):
    scaled = grad_rows * gain_row
    return inverse * (
        scaled
        - jnp.mean(scaled, axis=-1, keepdims=True)
        - normed * jnp.mean(scaled * normed, axis=-1, keepdims=True)
    )


def gelu_slope(pre_act):
    return (
        0.5 * (1.0 + lax.erf(pre_act * 0.7071067811865476))
        + pre_act * jnp.exp(-0.5 * pre_act * pre_act) * 0.3989422804014327
    )


def masked_scores(query_heads, key_heads, segment):
    scores = jnp.einsum(
        "qhd,khd->hqk", query_heads, key_heads, preferred_element_type=jnp.float32
    ) * HEAD_DIM ** (-0.5)
    same_block = segment[:, None] == segment[None, :]
    return jnp.where(same_block[None], scores, -1e30)


def split_heads(rows_low):
    return rows_low.reshape(rows_low.shape[0], HEADS, HEAD_DIM)


def attend(query_rows, key_rows, value_rows, segment):
    scores = masked_scores(split_heads(query_rows), split_heads(key_rows), segment)
    row_peak = jnp.max(scores, axis=-1, keepdims=True)
    exponent = jnp.exp(scores - row_peak)
    row_total = jnp.sum(exponent, axis=-1, keepdims=True)
    weights = (exponent / row_total).astype(jnp.bfloat16)
    log_total = row_peak + jnp.log(row_total)
    context = jnp.einsum(
        "hqk,khd->qhd", weights, split_heads(value_rows), preferred_element_type=jnp.float32
    )
    return (context.reshape(query_rows.shape).astype(jnp.bfloat16), log_total)


def attend_backward(query_rows, key_rows, value_rows, log_total, context_grad, segment):
    query_heads = split_heads(query_rows)
    key_heads = split_heads(key_rows)
    grad_heads = split_heads(context_grad)
    probabilities = jnp.exp(masked_scores(query_heads, key_heads, segment) - log_total)
    prob_low = probabilities.astype(jnp.bfloat16)
    value_grad = jnp.einsum(
        "hqk,qhd->khd", prob_low, grad_heads, preferred_element_type=jnp.float32
    )
    weight_grad = jnp.einsum(
        "qhd,khd->hqk", grad_heads, split_heads(value_rows), preferred_element_type=jnp.float32
    )
    row_inner = jnp.sum(probabilities * weight_grad, axis=-1, keepdims=True)
    score_low = (probabilities * (weight_grad - row_inner) * HEAD_DIM ** (-0.5)).astype(
        jnp.bfloat16
    )
    query_grad = jnp.einsum(
        "hqk,khd->qhd", score_low, key_heads, preferred_element_type=jnp.float32
    )
    key_grad = jnp.einsum(
        "hqk,qhd->khd", score_low, query_heads, preferred_element_type=jnp.float32
    )
    shape_out = query_rows.shape
    return (
        query_grad.reshape(shape_out),
        key_grad.reshape(shape_out),
        value_grad.reshape(shape_out),
    )


def layer_forward(params, rows_in, segment):
    w_qkv, w_out, w_in, w_down, biases, gains, bias_in = params
    model_width = w_out.shape[0]
    projected = jnp.dot(rows_in, w_qkv, preferred_element_type=jnp.float32)
    query_rows = (projected[:, :model_width] + biases[0]).astype(jnp.bfloat16)
    key_rows = projected[:, model_width : 2 * model_width].astype(jnp.bfloat16)
    value_rows = (projected[:, 2 * model_width :] + biases[1]).astype(jnp.bfloat16)
    context, log_total = jax.vmap(attend)(
        by_block(query_rows), by_block(key_rows), by_block(value_rows), segment.reshape(MICRO, SEQ)
    )
    context = context.reshape(rows_in.shape)
    first_sum = (
        rows_in.astype(jnp.float32)
        + jnp.dot(context, w_out, preferred_element_type=jnp.float32)
        + biases[2]
    )
    normed_out, first_normed, first_inverse = norm_forward(first_sum, gains[0], biases[3])
    normed_low = normed_out.astype(jnp.bfloat16)
    pre_act = jnp.dot(normed_low, w_in, preferred_element_type=jnp.float32) + bias_in
    activated = jax.nn.gelu(pre_act, approximate=False).astype(jnp.bfloat16)
    second_sum = (
        normed_out + jnp.dot(activated, w_down, preferred_element_type=jnp.float32) + biases[4]
    )
    result, second_normed, second_inverse = norm_forward(second_sum, gains[1], biases[5])
    kept_values = (
        rows_in,
        query_rows,
        key_rows,
        value_rows,
        log_total,
        context,
        first_normed,
        first_inverse,
        normed_low,
        pre_act,
        activated,
        second_normed,
        second_inverse,
        segment,
    )
    return (result.astype(jnp.bfloat16), kept_values)


def layer_backward(params, kept_values, cotangent):
    w_qkv, w_out, w_in, w_down, biases, gains, bias_in = params
    (
        rows_in,
        query_rows,
        key_rows,
        value_rows,
        log_total,
        context,
        first_normed,
        first_inverse,
        normed_low,
        pre_act,
        activated,
        second_normed,
        second_inverse,
        segment,
    ) = kept_values
    second_grad = norm_backward(cotangent, second_normed, second_inverse, gains[1])
    second_low = second_grad.astype(jnp.bfloat16)
    act_grad = jnp.dot(second_low, w_down.T, preferred_element_type=jnp.float32)
    pre_grad = act_grad * gelu_slope(pre_act)
    pre_low = pre_grad.astype(jnp.bfloat16)
    normed_grad = second_grad + jnp.dot(pre_low, w_in.T, preferred_element_type=jnp.float32)
    first_grad = norm_backward(normed_grad, first_normed, first_inverse, gains[0])
    first_low = first_grad.astype(jnp.bfloat16)
    context_grad = jnp.dot(first_low, w_out.T, preferred_element_type=jnp.float32).astype(
        jnp.bfloat16
    )
    query_grad, key_grad, value_grad = jax.vmap(attend_backward)(
        by_block(query_rows),
        by_block(key_rows),
        by_block(value_rows),
        log_total,
        by_block(context_grad),
        segment.reshape(MICRO, SEQ),
    )
    query_grad, key_grad, value_grad = (
        member.reshape(first_low.shape) for member in (query_grad, key_grad, value_grad)
    )
    joined = jnp.concatenate([query_grad, key_grad, value_grad], axis=1).astype(jnp.bfloat16)
    input_grad = first_grad + jnp.dot(joined, w_qkv.T, preferred_element_type=jnp.float32)
    bias_grads = jnp.stack(
        [
            jnp.sum(query_grad, axis=0),
            jnp.sum(value_grad, axis=0),
            jnp.sum(first_grad, axis=0),
            jnp.sum(normed_grad, axis=0),
            jnp.sum(second_grad, axis=0),
            jnp.sum(cotangent, axis=0),
        ]
    )
    gain_grads = jnp.stack(
        [jnp.sum(normed_grad * first_normed, axis=0), jnp.sum(cotangent * second_normed, axis=0)]
    )
    low_parts = (joined, first_low, pre_low, second_low)
    return (input_grad, low_parts, (bias_grads, gain_grads, jnp.sum(pre_grad, axis=0)))


def by_block(rows):
    return rows.reshape(MICRO, SEQ, rows.shape[-1])


def pack_small(biases, gains, bias_in):
    rows = jnp.concatenate([biases, gains, bias_in.reshape(4, TILE)], axis=0)
    return jnp.pad(rows, ((0, 4), (0, TILE)))


def unpack_small(gathered):
    rows = gathered.reshape(N_F, SMALL_ROWS, 2 * TILE)[:, :12, :TILE]
    wide = jnp.swapaxes(rows[:, :8], 0, 1).reshape(8, N_F * TILE)
    return wide[:6], wide[6:], rows[:, 8:].reshape(N_F * 4 * TILE)


def join_parts(part_qkv, part_out, part_in, part_down, small_sums):
    bias_grads, gain_grads, bias_in_grads = small_sums
    wide = jnp.concatenate([bias_grads, gain_grads], axis=0)
    small = jnp.concatenate(
        [
            jnp.swapaxes(wide.reshape(8, N_F, TILE), 0, 1),
            bias_in_grads.reshape(N_F, 4, TILE),
            jnp.zeros((N_F, 116, TILE), jnp.float32),
        ],
        axis=1,
    )
    down = jnp.swapaxes(part_down.reshape(N_F, 4, TILE, 1024), 1, 2)
    parts = [
        part_qkv.reshape(N_F, TILE, 3072),
        part_out.reshape(N_F, TILE, 1024),
        part_in.reshape(N_F, TILE, 4096),
        down.reshape(N_F, TILE, 4096),
        small.astype(jnp.bfloat16),
    ]
    return jnp.concatenate(parts, axis=2).reshape(4, 2, TILE, PAYLOAD)


def split_total(total):
    small = total[:, 12288:]
    return (
        total[:, :3072],
        total[:, 3072:4096],
        total[:, 4096:8192],
        jnp.swapaxes(total[:, 8192:12288].reshape(TILE, 4, 1024), 0, 1).reshape(512, 1024),
        small[:6],
        small[6:8],
        small[8:12].reshape(512),
    )


def body(ends_in, segment_ids, w_qkv, w_out, w_in, w_down, biases, gains, bias_in):
    section_index = lax.axis_index("section")
    is_first = section_index == 0
    local_rows = ends_in[0]
    gathered = gather_weights(
        w_qkv[0], w_out[0], w_in[0], w_down[0], pack_small(biases[0], gains[0], bias_in[0])
    )
    params = (*gathered[:4], *unpack_small(gathered[4]))
    early, _ = layer_forward(params, local_rows, segment_ids)
    carried = lax.ppermute(early, "section", [(0, 1)])
    result, kept_values = layer_forward(
        params, jnp.where(is_first, local_rows, carried), segment_ids
    )
    early_grad, _, _ = layer_backward(params, kept_values, local_rows.astype(jnp.float32))
    carried = lax.ppermute(early_grad.astype(jnp.bfloat16), "section", [(1, 0)])
    cotangent = jnp.where(is_first, carried, local_rows).astype(jnp.float32)
    backward, low_parts, small_sums = layer_backward(params, kept_values, cotangent)
    joined, first_low, pre_low, second_low = low_parts
    def weight_grad(rows, grads):
        return jnp.einsum(
            "ta,tb->ab", rows, grads, preferred_element_type=jnp.float32
        ).astype(jnp.bfloat16)

    parts = join_parts(
        weight_grad(kept_values[0], joined),
        weight_grad(kept_values[5], first_low),
        weight_grad(kept_values[8], pre_low),
        weight_grad(kept_values[10], second_low),
        small_sums,
    )
    total = reduce_parts(parts).astype(jnp.float32)
    ends_out = jnp.where(is_first, backward.astype(jnp.bfloat16), result)
    return tuple(member[None] for member in (ends_out, *split_total(total)))


def solution(mesh):
    in_specs = (
        P("section", ("fsdp", "replica"), None),
        P(("fsdp", "replica")),
        P("section", "fsdp", None),
        P("section", "fsdp", None),
        P("section", "fsdp", None),
        P("section", "fsdp", None),
        P("section", None, "fsdp"),
        P("section", None, "fsdp"),
        P("section", "fsdp"),
    )
    out_specs = (
        P("section", ("fsdp", "replica"), None),
        P("section", "fsdp", None),
        P("section", "fsdp", None),
        P("section", "fsdp", None),
        P("section", "fsdp", None),
        P("section", None, "fsdp"),
        P("section", None, "fsdp"),
        P("section", "fsdp"),
    )
    return jax.shard_map(body, mesh=mesh, in_specs=in_specs, out_specs=out_specs, check_vma=False)
```

time: 1330 us -> 550 us (0.41)
  waiting for transfers between devices: 645 us -> 26.4 us
  Pallas kernels: 0 us -> 199 us
  matrix products: 261 us -> 147 us
  other arithmetic: 116 us -> 19.1 us
  blocking collectives: 82.1 us -> 0 us
  local copies, waits for them, and re-layouts: 168 us -> 142 us
  starting transfers between devices: 23.4 us -> 6.19 us
  between operations: 17.7 us -> 1.53 us
    reduce_scatter x2 -> x0, waiting for transfers between devices: 274 us -> none  [the longest x1 245 us: body(): lax.psum_scatter(jnp.concatenate([part_qkv, part_out, part_in, part_down]...]
    psum x1 -> x0, waiting for transfers between devices: 239 us -> none  [body(): lax.psum((combined, small_parts[0], small_parts[1], small_parts[2]), 'rep...]
    pallas_call x0 -> x2, Pallas kernels: none -> 199 us  [the longest x1 124 us: reduce_parts(): pl.pallas_call(reduce_kernel, out_shape=jax.ShapeDtypeStruct((128, PAYLOA...]
    all_gather x4 -> x0, waiting for transfers between devices: 116 us -> none  [the longest x1 46.6 us: fetch_layer(): lax.all_gather(shards[2], 'fsdp', axis=0, tiled=True)]
    reshape x51 -> x8, local copies, waits for them, and re-layouts: 90.2 us -> 22 us  [the longest x6 11.9 us: layer_backward(): member.reshape(first_low.shape)]
    unnamed x384 -> x98, local copies, waits for them, and re-layouts: 14.7 us -> 49.1 us
    unnamed x53 -> x3, other arithmetic: 34.8 us -> 0.7 us
    all_gather x3 -> x0, blocking collectives: 33 us -> none  [the longest x1 12.1 us: fetch_layer(): lax.all_gather(shards[6], 'fsdp', axis=0, tiled=True)]
  transfers between devices with their start and end apart: 16 -> 2, of which waited for: 11 -> 2; matrix products, arithmetic and copies ran while one was open for 5% -> 0% of each run, Pallas kernels for 0% -> 0%
where the time goes in v1:
time: 550 us; the launch traced here: 541 us
  Pallas kernels  199 us (36%)
  matrix products  147 us (27%)
  local copies, waits for them, and re-layouts  142 us (26%)
  waiting for transfers between devices  26.4 us (5%)
  other arithmetic  19.1 us (3%)
  starting transfers between devices  6.19 us (1%)
    pallas_call x1, Pallas kernels, reduce_parts(): pl.pallas_call(reduce_kernel, out_shape=jax.ShapeDtypeStruct((128, PAYLOA...  124 us
    pallas_call x1, Pallas kernels, gather_weights(): pl.pallas_call(gather_kernel, out_shape=[jax.ShapeDtypeStruct((N_F * rows...  75.5 us
    unnamed x98, local copies, waits for them, and re-layouts  49.1 us
    dot_general x2, matrix products, layer_forward(): jnp.dot(activated, w_down, preferred_element_type=jnp.float32)  22.9 us
    another operation x10, local copies, waits for them, and re-layouts, split_heads(): return rows_low.reshape(rows_low.shape[0], HEADS, HEAD_DIM)  19.7 us
    dot_general x2, matrix products, layer_backward(): jnp.dot(pre_low, w_in.T, preferred_element_type=jnp.float32)  18.1 us
    ppermute x1, waiting for transfers between devices, body(): carried = lax.ppermute(early_grad.astype(jnp.bfloat16), 'section', [(1, 0)])  15.4 us
    dot_general x1, matrix products, layer_forward(): jnp.dot(normed_low, w_in, preferred_element_type=jnp.float32) + bias_in  14.9 us
  transfers between devices with their start and end apart: 2, of which 2 were waited for; matrix products, arithmetic and copies ran while one was open for 0% of the time, Pallas kernels for 0%

profile of v1, /device:TPU:6, one launch (start us, length us, event | category | flops | bytes accessed | tf_op | source)
XLA Modules:
  0.0 540.8 jit_solution(4581671068271473070)
XLA Ops:
  6.6 75.5 %gather_weights.1 = (bf16[1024,3072]{1,0:T(8,128)(2,1)S(1)}, bf16[1024,1024]{1,0:T(8,128)(2,1)S(1)}, bf16[1024,4096]{1,0:T(8,128)(2,1)S(1)}, bf16[4096,1024]{1,0:T(8,128)(2,1)S(1)}, bf16[128,256]{1,0:T(8,128)(2,1)S(1)}) custom-call(bf16[128,3072]{1,0:T(8,128)(2,1)S(1)} %bitcast.156, bf16[128,1024]{1,0:T(8,128)(2,1)S(1)} %bitcast.157, ...), custom_call_target="tpu_custom_call" | custom-call | tf_op jit(solution)/shard_map/gather_weights/pallas_call | solution.py:172
  82.1 3.2 copy-done.4
  85.3 3.2 copy-done.5
  92.1 4.8 convolution_bitcast_fusion
  104.7 3.9 fusion.270
  108.6 3.4 fusion.96
  118.8 20.4 %fusion.276 = (f32[256]{0:T(256)S(1)}, f32[256,1024]{1,0:T(8,128)}) fusion(f32[1024]{0:T(1024)S(1)} %bitcast.202, bf16[4096,1024]{1,0:T(8,128)(2,1)} %copy-done.5, bf16[1024,4096]{1,0:T(8,128)(2,1)} %copy-done.4, f32[4096]{0:T(1024)S(1)} %convert.102, f32[256,1024]{1,0:T(8,128)} %copy-done.35, f32[1024]{0:T(1024)S(1)} %bitcast.178, ...), kind=kOutput, calls=%fused_computation.342 | convolution fusion | flops 4367319040 | bytes 18906112 | tf_op jit(solution)/shard_map/dot_general | solution.py:485
  142.1 4.6 collective-permute-start
  146.8 11.1 %collective-permute-done = bf16[256,1024]{1,0:T(8,128)(2,1)} collective-permute-done((bf16[256,1024]{1,0:T(8,128)(2,1)S(1)}, bf16[256,1024]{1,0:T(8,128)(2,1)}, u32[]{:S(2)}, u32[]{:S(2)}) %collective-permute-start) | collective-permute-done | bytes 524320 | tf_op jit(solution)/shard_map/ppermute | solution.py:625
  157.9 4.8 fusion.286
  193.1 14.9 %fusion.9 = (bf16[256,4096]{1,0:T(8,128)(2,1)S(1)}, f32[256,4096]{1,0:T(8,128)}) fusion(f32[4096]{0:T(1024)S(1)} %convert.102, bf16[1024,4096]{1,0:T(8,128)(2,1)} %copy-done.4, f32[256,1024]{1,0:T(8,128)S(1)} %subtract_multiply_fusion.3, f32[1024]{0:T(1024)S(1)} %bitcast.179, f32[1024]{0:T(1024)S(1)} %bitcast.172), kind=kOutput, calls=%fused_computation.20 | convolution fusion | flops 2217476096 | bytes 15753216 | tf_op jit(solution)/shard_map/dot_general | solution.py:482
  211.9 15.5 %fusion.264 = (f32[256]{0:T(256)S(1)}, f32[256]{0:T(256)S(1)}, f32[256,1024]{1,0:T(8,128)}) fusion(f32[256,1024]{1,0:T(8,128)S(1)} %subtract_multiply_fusion.3, f32[1024]{0:T(1024)S(1)} %bitcast.174, bf16[1024,4096]{1,0:T(8,128)(2,1)} %copy-done.4, bf16[4096,1024]{1,0:T(8,128)(2,1)} %copy-done.5, bf16[1,256,1024]{2,1,0:T(8,128)(2,1)} %param.9, ...), kind=kOutput, calls=%fused_computation.335 | convolution fusion | flops 4311220224 | bytes 24655872 | tf_op jit(solution)/shard_map/dot_general | solution.py:530
  235.4 3.4 fusion.287
  240.5 6.0 %fusion.99 = bf16[4,64,16,64]{1,3,2,0:T(8,128)(2,1)} fusion(f32[4,16,64,64]{2,3,1,0:T(8,128)} %fusion.287, bf16[4,64,16,64]{1,0,3,2:T(4,128)(2,1)} %reshape_reshape.34, f32[4,16,64,64]{2,3,1,0:T(8,128)} %copy-done.8, f32[4,16,64]{2,1,0:T(8,128)S(1)} %log_add_fusion), kind=kOutput, calls=%fused_computation.129 | convolution fusion | flops 35655744 | bytes 3162112 | tf_op jit(solution)/shard_map/vmap(hqk,qhd->khd)/dot_general | solution.py:453
  246.5 6.0 %fusion.102 = bf16[4,64,16,64]{1,3,2,0:T(8,128)(2,1)} fusion(f32[4,16,64,64]{2,3,1,0:T(8,128)} %fusion.287, bf16[4,64,16,64]{3,2,1,0:T(8,128)(2,1)} %reshape_reshape.35, f32[4,16,64,64]{2,3,1,0:T(8,128)} %copy-done.8, f32[4,16,64]{2,1,0:T(8,128)S(1)} %log_add_fusion), kind=kOutput, calls=%fused_computation.130 | convolution fusion | flops 35655744 | bytes 3162112 | tf_op jit(solution)/shard_map/vmap(hqk,khd->qhd)/dot_general | solution.py:450
  268.6 5.5 %fusion.126 = bf16[256,1024]{1,0:T(8,128)(2,1)S(1)} fusion(bf16[1024,3072]{1,0:T(8,128)(2,1)} %copy-done.6, bf16[256,1024]{1,0:T(8,128)(2,1)} %reshape.290, bf16[256,1024]{1,0:T(8,128)(2,1)} %reshape.289, bf16[256,1024]{1,0:T(8,128)(2,1)} %reshape.288, f32[256,1024]{1,0:T(8,128)S(1)} %subtract_multiply_fusion.3, f32[256]{0:T(256)S(1)} %broadcast_multiply_fusion.4, ...), kind=kOutput, calls=%fused_computation.154 | convolution fusion | flops 1616904192 | bytes 10488832 | tf_op jit(solution)/shard_map/dot_general | solution.py:548
  275.7 15.4 %collective-permute-done.1 = bf16[256,1024]{1,0:T(8,128)(2,1)S(1)} collective-permute-done((bf16[256,1024]{1,0:T(8,128)(2,1)S(1)}, bf16[256,1024]{1,0:T(8,128)(2,1)S(1)}, u32[]{:S(2)}, u32[]{:S(2)}) %collective-permute-start.1) | collective-permute-done | bytes 524320 | tf_op jit(solution)/shard_map/ppermute | solution.py:630
  292.3 6.3 %fusion.285 = (bf16[4096]{0:T(1024)(128)(2,1)S(1)}, bf16[256,4096]{1,0:T(8,128)(2,1)S(1)}) fusion(f32[256,4096]{1,0:T(8,128)S(1)} %copy-done.36, bf16[4096,1024]{1,0:T(8,128)(2,1)} %copy-done.5, f32[256,1024]{1,0:T(8,128)S(1)} %get-tuple-element.48), kind=kOutput, calls=%fused_computation.345 | convolution fusion | flops 2159276032 | bytes 15736832 | tf_op jit(solution)/shard_map/dot_general | solution.py:527
  306.8 3.5 fusion.159
  310.4 5.4 %bitcast_convert_fusion.1 = (bf16[4,64,16,64]{3,1,2,0:T(8,128)(2,1)}, f32[4,16,64,64]{2,3,1,0:T(8,128)}) fusion(f32[4,16,64,64]{2,3,1,0:T(8,128)} %fusion.159, f32[4,16,64,64]{2,3,1,0:T(8,128)S(1)} %copy-done.10, f32[4,16,64]{2,1,0:T(8,128)S(1)} %log_add_fusion, bf16[4,64,16,64]{3,2,1,0:T(8,128)(2,1)} %reshape_reshape.35), kind=kOutput, calls=%fused_computation.61 | convolution fusion | flops 35655744 | bytes 4210688 | tf_op jit(solution)/shard_map/vmap(hqk,khd->qhd)/dot_general | solution.py:450
  315.8 4.5 fusion.105
  320.3 3.6 bitcast_convert_fusion
  336.9 6.3 %fusion.131 = bf16[1,256,1024]{2,1,0:T(8,128)(2,1)} fusion(f32[256,1024]{1,0:T(8,128)} %copy-done.16, bf16[256,3072]{1,0:T(8,128)(2,1)} %constant_dynamic-update-slice_fusion, bf16[1024,3072]{1,0:T(8,128)(2,1)} %copy-done.6, f32[1024]{0:T(1024)S(1)} %bitcast.200, f32[1024]{0:T(1024)S(1)} %bitcast.187, pred[]{:T(512)S(6)} %eq.14, ...), kind=kOutput, calls=%fused_computation.157 | convolution fusion | flops 1612709888 | bytes 10496001 | tf_op jit(solution)/shard_map/dot_general | solution.py:548
  347.2 5.6 %convolution_convert_fusion.1 = bf16[1024,4096]{1,0:T(8,128)(2,1)} fusion(bf16[256,4096]{1,0:T(8,128)(2,1)S(1)} %copy-done.33, f32[256,1024]{1,0:T(8,128)S(1)} %subtract_multiply_fusion.3, f32[1024]{0:T(1024)S(1)} %bitcast.181, f32[1024]{0:T(1024)S(1)} %bitcast.177), kind=kOutput, calls=%fused_computation.5 | convolution fusion | flops 2152464384 | bytes 11542528 | tf_op jit(solution)/shard_map/ta,tb->ab/dot_general | solution.py:635
  355.2 3.1 constant_dynamic-update-slice_fusion.14
  358.3 7.6 %copy.138 = bf16[8,4,128,1024]{3,1,2,0:T(4,128)(2,1)} copy(bf16[8,4,128,1024]{3,2,1,0:T(8,128)(2,1)S(1)} %bitcast.164) | data formatting | bytes 16777216 | tf_op jit(solution)/shard_map/reshape | solution.py:592
  365.9 14.5 %concatenate.59 = bf16[4,2,128,4096]{3,2,1,0:T(8,128)(2,1)} reshape(bf16[8,128,4,1024]{3,2,1,0:T(4,128)(2,1)} %bitcast.166) | data formatting | bytes 16777216 | tf_op jit(solution)/shard_map/concatenate | solution.py:600
  382.8 3.2 constant_dynamic-update-slice_fusion.13
  386.0 7.8 %constant_dynamic-update-slice_fusion.12 = bf16[4,2,128,12416]{3,2,1,0:T(8,128)(2,1)} fusion(bf16[4,2,128,12416]{3,2,1,0:T(8,128)(2,1)} %constant_dynamic-update-slice_fusion.13, bf16[4,2,128,4096]{3,2,1,0:T(8,128)(2,1)} %bitcast.165), kind=kLoop, calls=%fused_computation.252 | loop fusion | bytes 16777216
  393.8 7.8 %constant_dynamic-update-slice_fusion.11 = bf16[4,2,128,12416]{3,2,1,0:T(8,128)(2,1)} fusion(bf16[4,2,128,12416]{3,2,1,0:T(8,128)(2,1)} %constant_dynamic-update-slice_fusion.12, bf16[4,2,128,4096]{3,2,1,0:T(8,128)(2,1)} %concatenate.59), kind=kLoop, calls=%fused_computation.251 | loop fusion | bytes 16777216
  402.4 123.6 %reduce_parts.1 = bf16[128,12416]{1,0:T(8,128)(2,1)} custom-call(bf16[4,2,128,12416]{3,2,1,0:T(8,128)(2,1)} %maximum_dynamic-update-slice_fusion.parts), custom_call_target="tpu_custom_call" | custom-call | tf_op jit(solution)/shard_map/reduce_parts/pallas_call | solution.py:364
  535.9 4.1 copy.80
  (195 shorter events, 131.0 us)
Async XLA Ops:
  82.1 3.2 copy-start.4
  85.3 3.2 copy-start.5
  88.5 2.7 copy-start.6
  108.6 8.1 %copy-start.21 = (bf16[1,256,1024]{2,1,0:T(8,128)(2,1)S(1)}, bf16[1,256,1024]{2,1,0:T(8,128)(2,1)}, u32[]{:S(2)}) copy-start(bf16[1,256,1024]{2,1,0:T(8,128)(2,1)} %param.9) | copy-start | bytes 1572868
  142.1 15.7 %collective-permute-start = (bf16[256,1024]{1,0:T(8,128)(2,1)S(1)}, bf16[256,1024]{1,0:T(8,128)(2,1)}, u32[]{:S(2)}, u32[]{:S(2)}) collective-permute-start(bf16[256,1024]{1,0:T(8,128)(2,1)S(1)} %add_convert_fusion.3), channel_id=1, source_target_pairs={{0,64},{1,65},{2,66},{3,67},{4,68},{5,69},{6,70},{7,71},{8,72},{9,... | collective-permute-start | bytes 1572872 | tf_op jit(solution)/shard_map/ppermute | solution.py:625
  157.9 33.5 %copy-start.14 = (bf16[256,1024]{1,0:T(8,128)(2,1)}, bf16[256,1024]{1,0:T(8,128)(2,1)S(1)}, u32[]{:S(2)}) copy-start(bf16[256,1024]{1,0:T(8,128)(2,1)S(1)} %bitcast_select_fusion.1) | copy-start | bytes 1572868
  180.6 3.6 copy-start.18
  191.4 16.6 %slice-start.2 = ((s8[8388608]{0:T(1024)(128)(4,1)}), s8[4194304]{0:T(1024)(128)(4,1)S(1)}, s32[]{:S(2)}) async-start(s8[8388608]{0:T(1024)(128)(4,1)} %bitcast.162), calls=%async_computation.2 | async-start | bytes 8388608
  193.1 14.9 %slice-start.3 = ((s8[8388608]{0:T(1024)(128)(4,1)}), s8[4194304]{0:T(1024)(128)(4,1)S(1)}, s32[]{:S(2)}) async-start(s8[8388608]{0:T(1024)(128)(4,1)} %bitcast.162), calls=%async_computation.3 | async-start | bytes 8388608
  208.0 2.6 copy-start.26
  208.0 3.5 copy-start.22
  235.4 3.4 copy-start.9
  235.4 3.4 copy-start.19
  268.6 22.5 %copy-start.23 = (bf16[1,256,1024]{2,1,0:T(8,128)(2,1)S(1)}, bf16[1,256,1024]{2,1,0:T(8,128)(2,1)}, u32[]{:S(2)}) copy-start(bf16[1,256,1024]{2,1,0:T(8,128)(2,1)} %param.9) | copy-start | bytes 1572868
  268.6 22.7 %copy-start.12 = (f32[256,1024]{1,0:T(8,128)S(1)}, f32[256,1024]{1,0:T(8,128)}, u32[]{:S(2)}) copy-start(f32[256,1024]{1,0:T(8,128)} %copy-done.11) | copy-start | bytes 3145732
  274.1 18.2 %copy-start.36 = (f32[256,4096]{1,0:T(8,128)S(1)}, f32[256,4096]{1,0:T(8,128)}, u32[]{:S(2)}) copy-start(f32[256,4096]{1,0:T(8,128)} %get-tuple-element.74) | copy-start | bytes 12582916
  274.1 17.0 %collective-permute-start.1 = (bf16[256,1024]{1,0:T(8,128)(2,1)S(1)}, bf16[256,1024]{1,0:T(8,128)(2,1)S(1)}, u32[]{:S(2)}, u32[]{:S(2)}) collective-permute-start(bf16[256,1024]{1,0:T(8,128)(2,1)S(1)} %fusion.126), channel_id=1, source_target_pairs={{64,0},{65,1},{66,2},{67,3},{68,4},{69,5},{70,6},{71,7},{72,8},{73... | collective-permute-start | bytes 1572872 | tf_op jit(solution)/shard_map/ppermute | solution.py:630
  291.1 7.6 %slice-start = ((s8[8388608]{0:T(1024)(128)(4,1)}), s8[4194304]{0:T(1024)(128)(4,1)S(1)}, s32[]{:S(2)}) async-start(s8[8388608]{0:T(1024)(128)(4,1)} %bitcast.160), calls=%async_computation | async-start | bytes 8388608
  292.3 6.4 %copy-start.24 = (f32[256,1024]{1,0:T(8,128)}, f32[256,1024]{1,0:T(8,128)S(1)}, u32[]{:S(2)}) copy-start(f32[256,1024]{1,0:T(8,128)S(1)} %get-tuple-element.48) | copy-start | bytes 3145732
  292.3 6.4 %slice-start.1 = ((s8[8388608]{0:T(1024)(128)(4,1)}), s8[4194304]{0:T(1024)(128)(4,1)S(1)}, s32[]{:S(2)}) async-start(s8[8388608]{0:T(1024)(128)(4,1)} %bitcast.160), calls=%async_computation.1 | async-start | bytes 8388608
  298.6 2.7 copy-start.32
  304.2 6.2 %copy-start.10 = (f32[4,16,64,64]{2,3,1,0:T(8,128)S(1)}, f32[4,16,64,64]{2,3,1,0:T(8,128)}, u32[]{:S(2)}) copy-start(f32[4,16,64,64]{2,3,1,0:T(8,128)} %copy-done.8) | copy-start | bytes 3145732
  320.3 3.6 copy-start.34
  328.2 8.7 %copy-start.13 = (f32[256,1024]{1,0:T(8,128)S(1)}, f32[256,1024]{1,0:T(8,128)}, u32[]{:S(2)}) copy-start(f32[256,1024]{1,0:T(8,128)} %copy-done.11) | copy-start | bytes 3145732
  336.9 6.3 %copy-start.15 = (bf16[256,1024]{1,0:T(8,128)(2,1)S(1)}, bf16[256,1024]{1,0:T(8,128)(2,1)}, u32[]{:S(2)}) copy-start(bf16[256,1024]{1,0:T(8,128)(2,1)} %copy-done.14) | copy-start | bytes 1572868
  336.9 6.3 %copy-start.28 = (bf16[256,3072]{1,0:T(8,128)(2,1)S(1)}, bf16[256,3072]{1,0:T(8,128)(2,1)}, u32[]{:S(2)}) copy-start(bf16[256,3072]{1,0:T(8,128)(2,1)} %constant_dynamic-update-slice_fusion) | copy-start | bytes 4718596
  343.2 1.9 copy-start.31
  345.1 2.1 copy-start.33
  347.2 5.6 %copy-start.25 = (f32[256,1024]{1,0:T(8,128)S(1)}, f32[256,1024]{1,0:T(8,128)}, u32[]{:S(2)}) copy-start(f32[256,1024]{1,0:T(8,128)} %copy-done.24) | copy-start | bytes 3145732
  347.2 5.6 %copy-start.27 = (bf16[256,4096]{1,0:T(8,128)(2,1)S(1)}, bf16[256,4096]{1,0:T(8,128)(2,1)}, u32[]{:S(2)}) copy-start(bf16[256,4096]{1,0:T(8,128)(2,1)} %copy-done.26) | copy-start | bytes 6291460
  365.9 16.4 %copy-start.20 = (f32[4,16,64,64]{2,3,1,0:T(8,128)S(1)}, f32[4,16,64,64]{2,3,1,0:T(8,128)}, u32[]{:S(2)}) copy-start(f32[4,16,64,64]{2,3,1,0:T(8,128)} %get-tuple-element.82) | copy-start | bytes 3145732
  528.3 3.7 copy-start.7
  (11 other events, 13.5 us)

commit v2 on v1

--- a/solution.py
+++ b/solution.py
@@ -8,10 +8,6 @@
 HEADS = 16
 HEAD_DIM = 64
 SEQ = 64
-MICRO = 4
-
-
-EPSILON = 1e-05
 
 
 MESH = pl.DeviceIdType.MESH
@@ -383,221 +379,416 @@
     )(parts)
 
 
-def norm_forward(summed, gain_row, offset):
-    center = summed - jnp.mean(summed, axis=-1, keepdims=True)
-    inverse = lax.rsqrt(jnp.mean(center * center, axis=-1, keepdims=True) + EPSILON)
-    normed = center * inverse
-    return (normed * gain_row + offset, normed, inverse)
+EPSILON = 1e-05
+ROWS = 256
+WIDTH = 1024
+FF_WIDTH = 4096
+STRIP = 32
+FF_STEP = 512
+
+
+def dot(a, b):
+    return jnp.dot(a, b, preferred_element_type=jnp.float32)
+
+
+def dot_last(a, b):
+    return lax.dot_general(a, b, (((1,), (1,)), ((), ())), preferred_element_type=jnp.float32)
+
+
+def dot_first(a, b):
+    return lax.dot_general(a, b, (((0,), (0,)), ((), ())), preferred_element_type=jnp.float32)
+
+
+def row_mean(rows):
+    return jnp.mean(rows, axis=-1, keepdims=True)
+
+
+def norm_forward(summed):
+    center = summed - row_mean(summed)
+    inverse = lax.rsqrt(row_mean(center * center) + EPSILON)
+    return center * inverse, inverse
 
 
 def norm_backward(grad_rows, normed, inverse, gain_row):
     scaled = grad_rows * gain_row
-    return inverse * (
-        scaled
-        - jnp.mean(scaled, axis=-1, keepdims=True)
-        - normed * jnp.mean(scaled * normed, axis=-1, keepdims=True)
+    return inverse * (scaled - row_mean(scaled) - normed * row_mean(scaled * normed))
+
+
+def strips(body):
+    def one(n, carry):
+        body(pl.ds(pl.multiple_of(n * STRIP, STRIP), STRIP))
+        return carry
+
+    lax.fori_loop(0, ROWS // STRIP, one, 0)
+
+
+def layer_kernel(
+    ends,
+    id_column,
+    id_row,
+    w_qkv_far,
+    w_out_far,
+    w_in_far,
+    w_down_far,
+    small,
+    ends_out,
+    parts,
+    w_qkv,
+    w_out,
+    w_in,
+    w_down,
+    vec,
+    sums,
+    rows_in,
+    cotangent,
+    leaving,
+    qkv,
+    context,
+    first_normed,
+    first_inverse,
+    normed_out,
+    normed_low,
+    activated,
+    slope,
+    second_normed,
+    second_inverse,
+    chances,
+    second_low,
+    pre_low,
+    first_low,
+    joined,
+    total,
+    tiles,
+    small_rows,
+    small_tile,
+    load_sem,
+    store_sem,
+    send_sem,
+    recv_sem,
+):
+    section = lax.axis_index("section")
+    loads = [
+        pltpu.make_async_copy(far, near, load_sem.at[n])
+        for n, (far, near) in enumerate(
+            ((w_qkv_far, w_qkv), (w_out_far, w_out), (w_in_far, w_in), (w_down_far, w_down))
+        )
+    ]
+    for load in loads:
+        load.start()
+    other = {"section": 1 - section}
+    greet((other,))
+    onward = pltpu.make_async_remote_copy(
+        src_ref=leaving, dst_ref=rows_in, send_sem=send_sem.at[0], recv_sem=recv_sem.at[0],
+        device_id=other, device_id_type=MESH,
     )
-
-
-def gelu_slope(pre_act):
-    return (
-        0.5 * (1.0 + lax.erf(pre_act * 0.7071067811865476))
-        + pre_act * jnp.exp(-0.5 * pre_act * pre_act) * 0.3989422804014327
+    back = pltpu.make_async_remote_copy(
+        src_ref=leaving, dst_ref=cotangent, send_sem=send_sem.at[1], recv_sem=recv_sem.at[1],
+        device_id=other, device_id_type=MESH,
     )
-
-
-def masked_scores(query_heads, key_heads, segment):
-    scores = jnp.einsum(
-        "qhd,khd->hqk", query_heads, key_heads, preferred_element_type=jnp.float32
-    ) * HEAD_DIM ** (-0.5)
-    same_block = segment[:, None] == segment[None, :]
-    return jnp.where(same_block[None], scores, -1e30)
-
-
-def split_heads(rows_low):
-    return rows_low.reshape(rows_low.shape[0], HEADS, HEAD_DIM)
-
-
-def attend(query_rows, key_rows, value_rows, segment):
-    scores = masked_scores(split_heads(query_rows), split_heads(key_rows), segment)
-    row_peak = jnp.max(scores, axis=-1, keepdims=True)
-    exponent = jnp.exp(scores - row_peak)
-    row_total = jnp.sum(exponent, axis=-1, keepdims=True)
-    weights = (exponent / row_total).astype(jnp.bfloat16)
-    log_total = row_peak + jnp.log(row_total)
-    context = jnp.einsum(
-        "hqk,khd->qhd", weights, split_heads(value_rows), preferred_element_type=jnp.float32
+    for f in range(N_F):
+        shard = small[f * SMALL_ROWS : (f + 1) * SMALL_ROWS, :TILE].astype(jnp.float32)
+        vec[0:8, f * TILE : (f + 1) * TILE] = shard[0:8]
+        for i in range(4):
+            first = (f % 2) * 512 + i * TILE
+            vec[8 + f // 2 : 9 + f // 2, first : first + TILE] = shard[8 + i : 9 + i]
+    sums[...] = jnp.zeros_like(sums)
+    lane = lax.broadcasted_iota(jnp.int32, (1, TILE), 1)
+    head_masks = [
+        jnp.where((lane < HEAD_DIM) == (h == 0), 1.0, 0.0).astype(jnp.bfloat16) for h in (0, 1)
+    ]
+
+    @pl.when(section == 0)
+    def _():
+        rows_in[...] = ends[...]
+
+    @pl.when(section == 1)
+    def _():
+        cotangent[...] = ends[...]
+        onward.wait_recv()
+
+    loads[0].wait()
+    for j in range(6):
+        columns = slice(j * 512, (j + 1) * 512)
+        projected = dot(rows_in[...], w_qkv[:, columns])
+        if j // 2 != 1:
+            row = 0 if j < 2 else 1
+            first = (j % 2) * 512
+            projected = projected + vec[row : row + 1, first : first + 512]
+        qkv[:, columns] = projected.astype(jnp.bfloat16)
+
+    def head_columns(p, part):
+        return pl.ds(pl.multiple_of(part * WIDTH + p * TILE, TILE), TILE)
+
+    def attend(p, carry):
+        for b in (0, 1):
+            rows = slice(b * TILE, (b + 1) * TILE)
+            query = qkv[rows, head_columns(p, 0)]
+            key = qkv[rows, head_columns(p, 1)]
+            value = qkv[rows, head_columns(p, 2)]
+            same = id_column[rows, :] == id_row[:, rows]
+            mixed = None
+            for h in (0, 1):
+                scores = dot_last(query * head_masks[h], key) * HEAD_DIM ** (-0.5)
+                scores = jnp.where(same, scores, -1e30)
+                exponent = jnp.exp(scores - jnp.max(scores, axis=-1, keepdims=True))
+                share = exponent / jnp.sum(exponent, axis=-1, keepdims=True)
+                low = share.astype(jnp.bfloat16)
+                chances[p * 4 + b * 2 + h] = low
+                part = dot(low, value * head_masks[h])
+                mixed = part if mixed is None else mixed + part
+            context[rows, head_columns(p, 0)] = mixed.astype(jnp.bfloat16)
+        return carry
+
+    lax.fori_loop(0, HEADS // 2, attend, 0)
+    loads[1].wait()
+    total[...] = dot(context[...], w_out[...])
+
+    def first_norm(rows):
+        summed = rows_in[rows, :].astype(jnp.float32) + total[rows, :] + vec[2:3, :]
+        normed, inverse = norm_forward(summed)
+        first_normed[rows, :] = normed
+        first_inverse[rows, :] = jnp.broadcast_to(inverse, (STRIP, TILE))
+        shifted = normed * vec[6:7, :] + vec[3:4, :]
+        normed_out[rows, :] = shifted
+        normed_low[rows, :] = shifted.astype(jnp.bfloat16)
+
+    strips(first_norm)
+    loads[2].wait()
+    loads[3].wait()
+
+    def widen(j):
+        columns = slice(j * FF_STEP, (j + 1) * FF_STEP)
+        row, first = j * FF_STEP // WIDTH, j * FF_STEP % WIDTH
+        pre_act = dot(normed_low[...], w_in[:, columns])
+        pre_act = pre_act + vec[8 + row : 9 + row, first : first + FF_STEP]
+        phi = 0.5 * (1.0 + lax.erf(pre_act * 0.7071067811865476))
+        activated[:, columns] = (pre_act * phi).astype(jnp.bfloat16)
+        density = jnp.exp(-0.5 * pre_act * pre_act) * 0.3989422804014327
+        slope[:, columns] = (phi + pre_act * density).astype(jnp.bfloat16)
+
+    for j in range(FF_WIDTH // FF_STEP):
+        widen(j)
+    for n in range(2):
+        columns = slice(n * 512, (n + 1) * 512)
+        total[:, columns] = dot(activated[...], w_down[:, columns])
+
+    def second_norm(rows):
+        summed = normed_out[rows, :] + total[rows, :] + vec[4:5, :]
+        normed, inverse = norm_forward(summed)
+        second_normed[rows, :] = normed
+        second_inverse[rows, :] = jnp.broadcast_to(inverse, (STRIP, TILE))
+        leaving[rows, :] = (normed * vec[7:8, :] + vec[5:6, :]).astype(jnp.bfloat16)
+
+    strips(second_norm)
+
+    @pl.when(section == 0)
+    def _():
+        onward.start()
+        onward.wait_send()
+        back.wait_recv()
+
+    @pl.when(section == 1)
+    def _():
+        ends_out[...] = leaving[...]
+
+    def add_sum(row, values):
+        sums[row : row + 1, :] += jnp.sum(values, axis=0, keepdims=True)
+
+    def second_back(rows):
+        grad = cotangent[rows, :].astype(jnp.float32)
+        normed = second_normed[rows, :]
+        add_sum(5, grad)
+        add_sum(7, grad * normed)
+        grad = norm_backward(grad, normed, second_inverse[rows, 0:1], vec[7:8, :])
+        add_sum(4, grad)
+        normed_out[rows, :] = grad
+        second_low[rows, :] = grad.astype(jnp.bfloat16)
+
+    strips(second_back)
+    for j in range(FF_WIDTH // FF_STEP):
+        columns = slice(j * FF_STEP, (j + 1) * FF_STEP)
+        row, first = j * FF_STEP // WIDTH, j * FF_STEP % WIDTH
+        grad = dot_last(second_low[...], w_down[columns, :]) * slope[:, columns].astype(jnp.float32)
+        sums[8 + row : 9 + row, first : first + FF_STEP] = jnp.sum(grad, axis=0, keepdims=True)
+        pre_low[:, columns] = grad.astype(jnp.bfloat16)
+    for n in range(2):
+        columns = slice(n * 512, (n + 1) * 512)
+        total[:, columns] = dot_last(pre_low[...], w_in[columns, :])
+
+    def first_back(rows):
+        grad = normed_out[rows, :] + total[rows, :]
+        normed = first_normed[rows, :]
+        add_sum(3, grad)
+        add_sum(6, grad * normed)
+        grad = norm_backward(grad, normed, first_inverse[rows, 0:1], vec[6:7, :])
+        add_sum(2, grad)
+        normed_out[rows, :] = grad
+        first_low[rows, :] = grad.astype(jnp.bfloat16)
+
+    strips(first_back)
+    context_grad = leaving
+    for n in range(2):
+        columns = slice(n * 512, (n + 1) * 512)
+        context_grad[:, columns] = dot_last(first_low[...], w_out[columns, :]).astype(jnp.bfloat16)
+
+    def attend_back(p, carry):
+        for b in (0, 1):
+            rows = slice(b * TILE, (b + 1) * TILE)
+            query = qkv[rows, head_columns(p, 0)]
+            key = qkv[rows, head_columns(p, 1)]
+            value = qkv[rows, head_columns(p, 2)]
+            grads = context_grad[rows, head_columns(p, 0)]
+            results = [0.0, 0.0, 0.0]
+            for h in (0, 1):
+                own = grads * head_masks[h]
+                low = chances[p * 4 + b * 2 + h]
+                share = low.astype(jnp.float32)
+                weight_grad = dot_last(own, value)
+                inner = jnp.sum(share * weight_grad, axis=-1, keepdims=True)
+                score = (share * (weight_grad - inner) * HEAD_DIM ** (-0.5)).astype(jnp.bfloat16)
+                results[0] += dot(score, key * head_masks[h])
+                results[1] += dot_first(score, query * head_masks[h])
+                results[2] += dot_first(low, own)
+            for part in range(3):
+                joined[rows, head_columns(p, part)] = results[part].astype(jnp.bfloat16)
+            for row, part in ((0, 0), (1, 2)):
+                here = head_columns(p, 0)
+                sums[row : row + 1, here] += jnp.sum(results[part], axis=0, keepdims=True)
+        return carry
+
+    lax.fori_loop(0, HEADS // 2, attend_back, 0)
+    for n in range(2):
+        columns = slice(n * 512, (n + 1) * 512)
+        grad = normed_out[:, columns] + dot_last(joined[...], w_qkv[columns, :])
+        leaving[:, columns] = grad.astype(jnp.bfloat16)
+
+    @pl.when(section == 1)
+    def _():
+        back.start()
+
+    @pl.when(section == 0)
+    def _():
+        ends_out[...] = leaving[...]
+
+    for f in range(N_F):
+        small_rows[f, 0:8, :] = sums[0:8, f * TILE : (f + 1) * TILE]
+        for i in range(4):
+            first = (f % 2) * 512 + i * TILE
+            small_rows[f, 8 + i : 9 + i, :] = sums[8 + f // 2 : 9 + f // 2, first : first + TILE]
+        small_rows[f, 12:16, :] = jnp.zeros((4, TILE), jnp.float32)
+    small_tile[...] = jnp.zeros_like(small_tile)
+    for f in range(N_F):
+        small_tile[f // 2, f % 2, 0:16, :] = small_rows[f].astype(jnp.bfloat16)
+    small_copy = pltpu.make_async_copy(
+        small_tile, parts.at[:, :, :, 12 * WIDTH : 12 * WIDTH + TILE], store_sem.at[12]
     )
-    return (context.reshape(query_rows.shape).astype(jnp.bfloat16), log_total)
-
-
-def attend_backward(query_rows, key_rows, value_rows, log_total, context_grad, segment):
-    query_heads = split_heads(query_rows)
-    key_heads = split_heads(key_rows)
-    grad_heads = split_heads(context_grad)
-    probabilities = jnp.exp(masked_scores(query_heads, key_heads, segment) - log_total)
-    prob_low = probabilities.astype(jnp.bfloat16)
-    value_grad = jnp.einsum(
-        "hqk,qhd->khd", prob_low, grad_heads, preferred_element_type=jnp.float32
-    )
-    weight_grad = jnp.einsum(
-        "qhd,khd->hqk", grad_heads, split_heads(value_rows), preferred_element_type=jnp.float32
-    )
-    row_inner = jnp.sum(probabilities * weight_grad, axis=-1, keepdims=True)
-    score_low = (probabilities * (weight_grad - row_inner) * HEAD_DIM ** (-0.5)).astype(
-        jnp.bfloat16
-    )
-    query_grad = jnp.einsum(
-        "hqk,khd->qhd", score_low, key_heads, preferred_element_type=jnp.float32
-    )
-    key_grad = jnp.einsum(
-        "hqk,qhd->khd", score_low, query_heads, preferred_element_type=jnp.float32
-    )
-    shape_out = query_rows.shape
-    return (
-        query_grad.reshape(shape_out),
-        key_grad.reshape(shape_out),
-        value_grad.reshape(shape_out),
-    )
-
-
-def layer_forward(params, rows_in, segment):
-    w_qkv, w_out, w_in, w_down, biases, gains, bias_in = params
-    model_width = w_out.shape[0]
-    projected = jnp.dot(rows_in, w_qkv, preferred_element_type=jnp.float32)
-    query_rows = (projected[:, :model_width] + biases[0]).astype(jnp.bfloat16)
-    key_rows = projected[:, model_width : 2 * model_width].astype(jnp.bfloat16)
-    value_rows = (projected[:, 2 * model_width :] + biases[1]).astype(jnp.bfloat16)
-    context, log_total = jax.vmap(attend)(
-        by_block(query_rows), by_block(key_rows), by_block(value_rows), segment.reshape(MICRO, SEQ)
-    )
-    context = context.reshape(rows_in.shape)
-    first_sum = (
-        rows_in.astype(jnp.float32)
-        + jnp.dot(context, w_out, preferred_element_type=jnp.float32)
-        + biases[2]
-    )
-    normed_out, first_normed, first_inverse = norm_forward(first_sum, gains[0], biases[3])
-    normed_low = normed_out.astype(jnp.bfloat16)
-    pre_act = jnp.dot(normed_low, w_in, preferred_element_type=jnp.float32) + bias_in
-    activated = jax.nn.gelu(pre_act, approximate=False).astype(jnp.bfloat16)
-    second_sum = (
-        normed_out + jnp.dot(activated, w_down, preferred_element_type=jnp.float32) + biases[4]
-    )
-    result, second_normed, second_inverse = norm_forward(second_sum, gains[1], biases[5])
-    kept_values = (
-        rows_in,
-        query_rows,
-        key_rows,
-        value_rows,
-        log_total,
-        context,
-        first_normed,
-        first_inverse,
-        normed_low,
-        pre_act,
-        activated,
-        second_normed,
-        second_inverse,
-        segment,
-    )
-    return (result.astype(jnp.bfloat16), kept_values)
-
-
-def layer_backward(params, kept_values, cotangent):
-    w_qkv, w_out, w_in, w_down, biases, gains, bias_in = params
-    (
-        rows_in,
-        query_rows,
-        key_rows,
-        value_rows,
-        log_total,
-        context,
-        first_normed,
-        first_inverse,
-        normed_low,
-        pre_act,
-        activated,
-        second_normed,
-        second_inverse,
-        segment,
-    ) = kept_values
-    second_grad = norm_backward(cotangent, second_normed, second_inverse, gains[1])
-    second_low = second_grad.astype(jnp.bfloat16)
-    act_grad = jnp.dot(second_low, w_down.T, preferred_element_type=jnp.float32)
-    pre_grad = act_grad * gelu_slope(pre_act)
-    pre_low = pre_grad.astype(jnp.bfloat16)
-    normed_grad = second_grad + jnp.dot(pre_low, w_in.T, preferred_element_type=jnp.float32)
-    first_grad = norm_backward(normed_grad, first_normed, first_inverse, gains[0])
-    first_low = first_grad.astype(jnp.bfloat16)
-    context_grad = jnp.dot(first_low, w_out.T, preferred_element_type=jnp.float32).astype(
-        jnp.bfloat16
-    )
-    query_grad, key_grad, value_grad = jax.vmap(attend_backward)(
-        by_block(query_rows),
-        by_block(key_rows),
-        by_block(value_rows),
-        log_total,
-        by_block(context_grad),
-        segment.reshape(MICRO, SEQ),
-    )
-    query_grad, key_grad, value_grad = (
-        member.reshape(first_low.shape) for member in (query_grad, key_grad, value_grad)
-    )
-    joined = jnp.concatenate([query_grad, key_grad, value_grad], axis=1).astype(jnp.bfloat16)
-    input_grad = first_grad + jnp.dot(joined, w_qkv.T, preferred_element_type=jnp.float32)
-    bias_grads = jnp.stack(
-        [
-            jnp.sum(query_grad, axis=0),
-            jnp.sum(value_grad, axis=0),
-            jnp.sum(first_grad, axis=0),
-            jnp.sum(normed_grad, axis=0),
-            jnp.sum(second_grad, axis=0),
-            jnp.sum(cotangent, axis=0),
-        ]
-    )
-    gain_grads = jnp.stack(
-        [jnp.sum(normed_grad * first_normed, axis=0), jnp.sum(cotangent * second_normed, axis=0)]
-    )
-    low_parts = (joined, first_low, pre_low, second_low)
-    return (input_grad, low_parts, (bias_grads, gain_grads, jnp.sum(pre_grad, axis=0)))
-
-
-def by_block(rows):
-    return rows.reshape(MICRO, SEQ, rows.shape[-1])
+    small_copy.start()
+
+    def store(slot, y):
+        return pltpu.make_async_copy(
+            tiles.at[slot],
+            parts.at[y, :, :, slot * WIDTH : (slot + 1) * WIDTH],
+            store_sem.at[slot],
+        )
+
+    def weight_grads(y, carry):
+        block = pl.ds(pl.multiple_of(y * 256, 256), 256)
+
+        @pl.when(y > 0)
+        def _():
+            for slot in range(12):
+                store(slot, y - 1).wait()
+
+        for slot in range(8):
+            if slot < 3:
+                left, right, column = rows_in, joined, slot
+            elif slot == 3:
+                left, right, column = context, first_low, 0
+            else:
+                left, right, column = normed_low, pre_low, slot - 4
+            tile = dot_first(left[:, block], right[:, column * WIDTH : (column + 1) * WIDTH])
+            tiles[slot] = tile.astype(jnp.bfloat16).reshape(2, TILE, WIDTH)
+            store(slot, y).start()
+        for core in (0, 1):
+            for pair in (0, 1):
+                first = pl.multiple_of(y * WIDTH + core * 512 + pair * 256, 256)
+                tile = dot_first(activated[:, pl.ds(first, 256)], second_low[...])
+                low = tile.astype(jnp.bfloat16)
+                tiles[8 + 2 * pair, core] = low[:TILE]
+                tiles[9 + 2 * pair, core] = low[TILE:]
+        for slot in range(8, 12):
+            store(slot, y).start()
+        return carry
+
+    lax.fori_loop(0, 4, weight_grads, 0)
+    for slot in range(12):
+        store(slot, 3).wait()
+    small_copy.wait()
+
+    @pl.when(section == 1)
+    def _():
+        back.wait_send()
+
+
+def run_layer(ends, ids, weights, small):
+    low, full = jnp.bfloat16, jnp.float32
+    scratch = [
+        ((1024, 3072), low),
+        ((1024, 1024), low),
+        ((1024, 4096), low),
+        ((4096, 1024), low),
+        ((16, WIDTH), full),
+        ((16, WIDTH), full),
+        ((ROWS, WIDTH), low),
+        ((ROWS, WIDTH), low),
+        ((ROWS, WIDTH), low),
+        ((ROWS, 3 * WIDTH), low),
+        ((ROWS, WIDTH), low),
+        ((ROWS, WIDTH), full),
+        ((ROWS, TILE), full),
+        ((ROWS, WIDTH), full),
+        ((ROWS, WIDTH), low),
+        ((ROWS, FF_WIDTH), low),
+        ((ROWS, FF_WIDTH), low),
+        ((ROWS, WIDTH), full),
+        ((ROWS, TILE), full),
+        ((2 * HEADS, TILE, TILE), low),
+        ((ROWS, WIDTH), low),
+        ((ROWS, FF_WIDTH), low),
+        ((ROWS, WIDTH), low),
+        ((ROWS, 3 * WIDTH), low),
+        ((ROWS, WIDTH), full),
+        ((12, 2, TILE, WIDTH), low),
+        ((N_F, SMALL_ROWS, TILE), full),
+        ((4, 2, TILE, TILE), low),
+    ]
+    near = pl.BlockSpec(memory_space=pltpu.VMEM)
+    far = pl.BlockSpec(memory_space=pl.ANY)
+    return pl.pallas_call(
+        layer_kernel,
+        out_shape=[
+            jax.ShapeDtypeStruct((ROWS, WIDTH), low),
+            jax.ShapeDtypeStruct((4, 2, TILE, PAYLOAD), low),
+        ],
+        in_specs=[near, near, near, far, far, far, far, near],
+        out_specs=[near, far],
+        scratch_shapes=[
+            *[pltpu.VMEM(shape, kind) for shape, kind in scratch],
+            pltpu.SemaphoreType.DMA((4,)),
+            pltpu.SemaphoreType.DMA((13,)),
+            pltpu.SemaphoreType.DMA((2,)),
+            pltpu.SemaphoreType.DMA((2,)),
+        ],
+        compiler_params=pltpu.CompilerParams(
+            collective_id=2, has_side_effects=True, vmem_limit_bytes=VMEM_CAP
+        ),
+        name="run_layer",
+    )(ends, ids[:, None], ids[None, :], *weights, small)
 
 
 def pack_small(biases, gains, bias_in):
     rows = jnp.concatenate([biases, gains, bias_in.reshape(4, TILE)], axis=0)
     return jnp.pad(rows, ((0, 4), (0, TILE)))
-
-
-def unpack_small(gathered):
-    rows = gathered.reshape(N_F, SMALL_ROWS, 2 * TILE)[:, :12, :TILE]
-    wide = jnp.swapaxes(rows[:, :8], 0, 1).reshape(8, N_F * TILE)
-    return wide[:6], wide[6:], rows[:, 8:].reshape(N_F * 4 * TILE)
-
-
-def join_parts(part_qkv, part_out, part_in, part_down, small_sums):
-    bias_grads, gain_grads, bias_in_grads = small_sums
-    wide = jnp.concatenate([bias_grads, gain_grads], axis=0)
-    small = jnp.concatenate(
-        [
-            jnp.swapaxes(wide.reshape(8, N_F, TILE), 0, 1),
-            bias_in_grads.reshape(N_F, 4, TILE),
-            jnp.zeros((N_F, 116, TILE), jnp.float32),
-        ],
-        axis=1,
-    )
-    down = jnp.swapaxes(part_down.reshape(N_F, 4, TILE, 1024), 1, 2)
-    parts = [
-        part_qkv.reshape(N_F, TILE, 3072),
-        part_out.reshape(N_F, TILE, 1024),
-        part_in.reshape(N_F, TILE, 4096),
-        down.reshape(N_F, TILE, 4096),
-        small.astype(jnp.bfloat16),
-    ]
-    return jnp.concatenate(parts, axis=2).reshape(4, 2, TILE, PAYLOAD)
 
 
 def split_total(total):
@@ -614,37 +805,12 @@
 
 
 def body(ends_in, segment_ids, w_qkv, w_out, w_in, w_down, biases, gains, bias_in):
-    section_index = lax.axis_index("section")
-    is_first = section_index == 0
-    local_rows = ends_in[0]
     gathered = gather_weights(
         w_qkv[0], w_out[0], w_in[0], w_down[0], pack_small(biases[0], gains[0], bias_in[0])
     )
-    params = (*gathered[:4], *unpack_small(gathered[4]))
-    early, _ = layer_forward(params, local_rows, segment_ids)
-    carried = lax.ppermute(early, "section", [(0, 1)])
-    result, kept_values = layer_forward(
-        params, jnp.where(is_first, local_rows, carried), segment_ids
-    )
-    early_grad, _, _ = layer_backward(params, kept_values, local_rows.astype(jnp.float32))
-    carried = lax.ppermute(early_grad.astype(jnp.bfloat16), "section", [(1, 0)])
-    cotangent = jnp.where(is_first, carried, local_rows).astype(jnp.float32)
-    backward, low_parts, small_sums = layer_backward(params, kept_values, cotangent)
-    joined, first_low, pre_low, second_low = low_parts
-    def weight_grad(rows, grads):
-        return jnp.einsum(
-            "ta,tb->ab", rows, grads, preferred_element_type=jnp.float32
-        ).astype(jnp.bfloat16)
-
-    parts = join_parts(
-        weight_grad(kept_values[0], joined),
-        weight_grad(kept_values[5], first_low),
-        weight_grad(kept_values[8], pre_low),
-        weight_grad(kept_values[10], second_low),
-        small_sums,
-    )
+    ids = segment_ids + (lax.iota(jnp.int32, ROWS) // SEQ) * 16
+    ends_out, parts = run_layer(ends_in[0], ids, gathered[:4], gathered[4])
     total = reduce_parts(parts).astype(jnp.float32)
-    ends_out = jnp.where(is_first, backward.astype(jnp.bfloat16), result)
     return tuple(member[None] for member in (ends_out, *split_total(total)))
 
 

time: 550 us -> 351 us (0.64); the launches traced: 541 us -> 349 us
  matrix products: 147 us -> 0 us
  Pallas kernels: 199 us -> 312 us
  local copies, waits for them, and re-layouts: 142 us -> 34 us
  waiting for transfers between devices: 26.4 us -> 0 us
  other arithmetic: 19.1 us -> 2.5 us
  starting transfers between devices: 6.19 us -> 0 us
    dot_general x29 -> x0, matrix products: 143 us -> none  [the longest x2 22.9 us: layer_forward(): jnp.dot(activated, w_down, preferred_element_type=jnp.float32)]
    pallas_call x0 -> x1, Pallas kernels: none -> 113 us  [run_layer(): pl.pallas_call(layer_kernel, out_shape=[jax.ShapeDtypeStruct((ROWS, WIDTH...]
    unnamed x98 -> x26, local copies, waits for them, and re-layouts: 49.1 us -> 17 us
    ppermute x2 -> x0, waiting for transfers between devices: 26.4 us -> none  [the longest x1 15.4 us: body(): carried = lax.ppermute(early_grad.astype(jnp.bfloat16), 'section', [(1, 0)])]
    another operation x12 -> x0, local copies, waits for them, and re-layouts: 22.3 us -> none  [the longest x10 19.7 us: split_heads(): return rows_low.reshape(rows_low.shape[0], HEADS, HEAD_DIM)]
    reshape x7 -> x0, local copies, waits for them, and re-layouts: 19.5 us -> none  [the longest x6 11.9 us: layer_backward(): member.reshape(first_low.shape)]
    concatenate x6 -> x0, local copies, waits for them, and re-layouts: 16.6 us -> none  [the longest x1 14.5 us: join_parts(): return jnp.concatenate(parts, axis=2).reshape(4, 2, TILE, PAYLOAD)]
    transpose x6 -> x0, local copies, waits for them, and re-layouts: 10 us -> none  [the longest x2 4.75 us: attend_backward(): jnp.einsum('hqk,qhd->khd', score_low, query_heads, preferred_element_type...]
  transfers between devices with their start and end apart: 2 -> 0, of which waited for: 2 -> 0; matrix products, arithmetic and copies ran while one was open for 0% -> 0% of each run, Pallas kernels for 0% -> 0%
where the time goes in v2:
time: 351 us; the launch traced here: 349 us
  Pallas kernels  312 us (89%)
  local copies, waits for them, and re-layouts  34 us (10%)
    pallas_call x1, Pallas kernels, reduce_parts(): pl.pallas_call(reduce_kernel, out_shape=jax.ShapeDtypeStruct((128, PAYLOA...  123 us
    pallas_call x1, Pallas kernels, run_layer(): pl.pallas_call(layer_kernel, out_shape=[jax.ShapeDtypeStruct((ROWS, WIDTH...  113 us
    pallas_call x1, Pallas kernels, gather_weights(): pl.pallas_call(gather_kernel, out_shape=[jax.ShapeDtypeStruct((N_F * rows...  75.5 us
    unnamed x26, local copies, waits for them, and re-layouts  17 us

profile of v2, /device:TPU:6, one launch (start us, length us, event | category | flops | bytes accessed | tf_op | source)
XLA Modules:
  0.0 348.7 jit_solution(462375196119154393)
XLA Ops:
  0.6 0.7 fusion.10
  1.3 0.7 reduce
  2.0 0.7 fusion.8.refs_4_
  2.7 0.8 copy.19.id_column
  3.5 1.2 copy-done.4
  4.8 1.2 copy-done.5
  6.0 1.1 copy-done.6
  7.1 0.9 copy-done.7
  8.1 75.5 %gather_weights.1 = (bf16[1024,3072]{1,0:T(8,128)(2,1)S(1)}, bf16[1024,1024]{1,0:T(8,128)(2,1)S(1)}, bf16[1024,4096]{1,0:T(8,128)(2,1)S(1)}, bf16[4096,1024]{1,0:T(8,128)(2,1)S(1)}, bf16[128,256]{1,0:T(8,128)(2,1)S(1)}) custom-call(bf16[128,3072]{1,0:T(8,128)(2,1)S(1)} %bitcast.26, bf16[128,1024]{1,0:T(8,128)(2,1)S(1)} %bitcast.27, ...), custom_call_target="tpu_custom_call" | custom-call | tf_op jit(solution)/shard_map/gather_weights/pallas_call | solution.py:168
  83.5 0.0 copy-start
  83.6 3.2 copy-done
  86.8 3.2 copy-done.1
  90.0 2.7 copy-done.2
  92.7 1.3 copy-done.3
  94.0 0.6 copy-done.8
  94.7 0.0 copy-done.11
  94.7 113.2 %run_layer.1 = (bf16[256,1024]{1,0:T(8,128)(2,1)}, bf16[4,2,128,12416]{3,2,1,0:T(8,128)(2,1)}) custom-call(bf16[256,1024]{1,0:T(8,128)(2,1)} %bitcast.30, s32[256,1]{1,0:T(8,128)} %copy.19.id_column, s32[1,256]{1,0:T(1,128)} %bitcast.33, bf16[1024,3072]{1,0:T(8,128)(2,1)} %copy-done.2, bf16[1024,1024]{1,0:T(8,128)(2,1)} %copy-done.3, ...), custom_call_target="tpu_custom_call" | custom-call | tf_op jit(solution)/shard_map/run_layer/pallas_call | solution.py:767
  207.8 122.9 %reduce_parts.1 = bf16[128,12416]{1,0:T(8,128)(2,1)} custom-call(bf16[4,2,128,12416]{3,2,1,0:T(8,128)(2,1)} %get-tuple-element.21.parts), custom_call_target="tpu_custom_call" | custom-call | tf_op jit(solution)/shard_map/reduce_parts/pallas_call | solution.py:360
  330.8 1.3 slice.38
  332.0 2.9 slice.35
  334.9 3.6 %reshape.19 = f32[128,4,1024]{2,1,0:T(4,128)} reshape(f32[128,4096]{1,0:T(8,128)} %slice.35) | data formatting | bytes 4194304 | tf_op jit(solution)/shard_map/reshape | solution.py:800
  338.5 4.1 %copy.20 = f32[4,128,1024]{2,1,0:T(8,128)} copy(f32[4,128,1024]{2,0,1:T(4,128)} %bitcast.28) | data formatting | bytes 4194304 | tf_op jit(solution)/shard_map/transpose | solution.py:800
  342.7 0.0 copy-done.9
  342.7 0.4 convert_element_type.5
  343.1 0.0 copy-start.10
  343.1 0.6 slice_bitcast_fusion.4
  343.7 0.6 copy.21
  344.3 0.8 slice_bitcast_fusion.2
  345.1 1.3 slice_bitcast_fusion.1
  346.4 1.5 slice_bitcast_fusion
  347.9 0.0 copy-done.10
  348.0 0.8 copy.23
  (11 shorter events, 0.0 us)
Async XLA Ops:
  1.3 93.4 %copy-start.11 = (s32[256]{0:T(256)}, s32[256]{0:T(256)S(1)}, u32[]{:S(2)}) copy-start(s32[256]{0:T(256)S(1)} %fusion.10) | copy-start | bytes 3076
  3.5 1.2 copy-start.4
  4.8 1.2 copy-start.5
  6.0 1.1 copy-start.6
  7.1 0.9 copy-start.7
  83.5 3.2 copy-start
  86.8 3.2 copy-start.1
  90.0 2.7 copy-start.2
  92.7 1.3 copy-start.3
  94.0 0.6 copy-start.8
  332.0 10.7 %copy-start.9 = (bf16[128,12416]{1,0:T(8,128)(2,1)S(1)}, bf16[128,12416]{1,0:T(8,128)(2,1)}, u32[]{:S(2)}) copy-start(bf16[128,12416]{1,0:T(8,128)(2,1)} %reduce_parts.1) | copy-start | bytes 9535492
  343.1 4.9 %copy-start.10 = (bf16[256,1024]{1,0:T(8,128)(2,1)S(1)}, bf16[256,1024]{1,0:T(8,128)(2,1)}, u32[]{:S(2)}) copy-start(bf16[256,1024]{1,0:T(8,128)(2,1)} %get-tuple-element.20) | copy-start | bytes 1572868

commit v3 on v2

--- a/solution.py
+++ b/solution.py
@@ -8,12 +8,31 @@
 HEADS = 16
 HEAD_DIM = 64
 SEQ = 64
+EPSILON = 1e-05
+ROWS = 256
+WIDTH = 1024
+FF_WIDTH = 4096
+STRIP = 32
+FF_STEP = 512
+
+
+def dot(a, b):
+    return jnp.dot(a, b, preferred_element_type=jnp.float32)
+
+
+def dot_last(a, b):
+    return lax.dot_general(a, b, (((1,), (1,)), ((), ())), preferred_element_type=jnp.float32)
+
+
+def dot_first(a, b):
+    return lax.dot_general(a, b, (((0,), (0,)), ((), ())), preferred_element_type=jnp.float32)
 
 
 MESH = pl.DeviceIdType.MESH
 N_F = 8
 TILE = 128
 SMALL_ROWS = 16
+GATHER_COPIES = 112
 PAYLOAD = 97 * TILE
 VMEM_CAP = 60 * 1024 * 1024
 
@@ -43,37 +62,44 @@
 
 class Copies:
     def __init__(self, send_sem, recv_sem):
-        self.send_sem, self.recv_sem, self.started = send_sem, recv_sem, []
+        self.send_sem, self.recv_sem, self.count, self.unsent = send_sem, recv_sem, 0, []
 
     def start(self, src, dst, peer):
-        number = len(self.started)
         copy = pltpu.make_async_remote_copy(
             src_ref=src,
             dst_ref=dst,
-            send_sem=self.send_sem.at[number],
-            recv_sem=self.recv_sem.at[number],
+            send_sem=self.send_sem.at[self.count],
+            recv_sem=self.recv_sem.at[self.count],
             device_id=peer,
             device_id_type=MESH,
         )
         copy.start()
-        self.started.append(copy)
+        self.count += 1
+        self.unsent.append(copy)
         return copy
 
+    def sent(self, copy):
+        copy.wait_send()
+        self.unsent = [member for member in self.unsent if member is not copy]
+
     def finish(self):
-        for copy in self.started:
+        for copy in self.unsent:
             copy.wait_send()
 
 
-def gather_kernel(*refs):
+def gather_into(ins, outs, copies, local_sem, others):
     count = len(GATHER_PLAN)
-    ins, outs = refs[:count], refs[count : 2 * count]
-    send_sem, recv_sem, local_sem = refs[2 * count :]
     y, c, x, z = place()
     right_y, left_y = device(step_on(y, 1), c, x, z), device(step_on(y, -1), c, x, z)
     right_x, left_x = device(y, c, step_on(x, 1), z), device(y, c, step_on(x, -1), z)
     sibling = device(y, 1 - c, x, z)
-    greet((right_y, left_y, right_x, left_x, sibling))
-    copies = Copies(send_sem, recv_sem)
+    own = []
+    for k in range(count):
+        start = pl.multiple_of((y * 2 + c) * GATHER_PLAN[k][0], 16)
+        here = outs[k].at[pl.ds(start, GATHER_PLAN[k][0]), :]
+        own.append(pltpu.make_async_copy(ins[k], here, local_sem.at[k]))
+        own[-1].start()
+    greet((right_y, left_y, right_x, left_x, sibling, *others))
 
     def span(k, owner_y, first, rows, part=None):
         shard_rows, columns, _ = GATHER_PLAN[k]
@@ -88,7 +114,7 @@
 
     relayed = [k for k in range(count) if GATHER_PLAN[k][2]]
     direct = [k for k in range(count) if GATHER_PLAN[k][0] > 4 * GATHER_PLAN[k][2]]
-    first_right, first_left = {}, {}
+    first_right, first_left, loaded = {}, {}, []
     for kind, members in (("relay", relayed), ("direct", direct)):
         for k in members:
             shard_rows, _, piece = GATHER_PLAN[k]
@@ -96,16 +122,16 @@
                 first, rows = quarter(k, x), piece
             else:
                 first, rows = 4 * piece, shard_rows - 4 * piece
-            src = ins[k].at[pl.ds(first, rows), :]
-            first_right[kind, k] = copies.start(src, span(k, y, first, rows), right_y)
-            first_left[kind, k] = copies.start(src, span(k, y, first, rows), left_y)
-    own = []
-    sibling_copies = []
+            if k not in loaded:
+                own[k].wait()
+                loaded.append(k)
+            src = span(k, y, first, rows)
+            first_right[kind, k] = copies.start(src, src, right_y)
+            first_left[kind, k] = copies.start(src, src, left_y)
+    sibling_copies = {}
     for k in range(count):
-        shard_rows = GATHER_PLAN[k][0]
-        own.append(pltpu.make_async_copy(ins[k], span(k, y, 0, shard_rows), local_sem.at[k]))
-        own[-1].start()
-        sibling_copies.append(copies.start(ins[k], span(k, y, 0, shard_rows), sibling))
+        block = span(k, y, 0, GATHER_PLAN[k][0])
+        sibling_copies[3, k] = copies.start(block, block, sibling)
 
     before, after, across = step_on(y, -1), step_on(y, 1), step_on(y, 2)
     second_right, second_left = {}, {}
@@ -145,85 +171,67 @@
             along_left[n, k].wait_recv()
             block = span(k, owners[n], quarter(k, step_on(x, 1)), piece, 1)
             further[n, k, 1] = copies.start(block, block, left_x)
-    for n in range(3):
-        for k in range(count):
-            shard_rows = GATHER_PLAN[k][0]
+    for k in range(count):
+        for n in range(3):
             if n == 2 and k in direct:
                 second_right["direct", k].wait_recv()
                 second_left["direct", k].wait_recv()
             if k in relayed:
                 further[n, k, 0].wait_recv()
                 further[n, k, 1].wait_recv()
-            block = span(k, owners[n], 0, shard_rows)
-            sibling_copies.append(copies.start(block, block, sibling))
-    for copy in own:
-        copy.wait()
-    for copy in sibling_copies:
-        copy.wait_recv()
-    copies.finish()
-
-
-def gather_weights(*shards):
-    copies = 160
-    return pl.pallas_call(
-        gather_kernel,
-        out_shape=[
-            jax.ShapeDtypeStruct((N_F * rows, columns), jnp.bfloat16)
-            for rows, columns, _ in GATHER_PLAN
-        ],
-        in_specs=[pl.BlockSpec(memory_space=pl.ANY)] * len(GATHER_PLAN),
-        out_specs=[pl.BlockSpec(memory_space=pl.ANY)] * len(GATHER_PLAN),
-        scratch_shapes=[
-            pltpu.SemaphoreType.DMA((copies,)),
-            pltpu.SemaphoreType.DMA((copies,)),
-            pltpu.SemaphoreType.DMA((len(GATHER_PLAN),)),
-        ],
-        compiler_params=pltpu.CompilerParams(
-            collective_id=0, has_side_effects=True, vmem_limit_bytes=4 * 1024 * 1024
-        ),
-        name="gather_weights",
-    )(*shards)
-
-
-REDUCE_PLAN = ((8, 8, "y"), (8, 8, "x"), (8, 8, "y"), (8, 8, "y"), (8, 8, "x"), (8, 9, "y"))
+            block = span(k, owners[n], 0, GATHER_PLAN[k][0])
+            sibling_copies[n, k] = copies.start(block, block, sibling)
+
+    def arrived(k):
+        for n in range(4):
+            sibling_copies[n, k].wait_recv()
+
+    return arrived
+
+
+REDUCE_PLAN = ((4, 2, "y"), (6, 2, "x"), (0, 2, "y"), (2, 2, "y"), (8, 2, "x"), (10, 2, "y"))
+UNITS = 12
+
+
+def chunk_width(plan):
+    first, units, _ = plan
+    return units * WIDTH + (TILE if first + units == UNITS else 0)
 
 
 def stage_shape(plan, stage):
-    part_a, part_b, leading = plan
-    rows = {("y", 0): (1, 128), ("x", 0): (4, 32), ("y", 1): (1, 32), ("x", 1): (1, 32)}
-    blocks, height = rows[leading, stage]
-    return blocks, height, (part_a + part_b) * TILE
-
-
-def add_into(target, rows, columns, sources, dest=None):
-    blocks, first_block, height, first_row = rows
-    first_column, width = columns
-
+    shapes = {("y", 0): (1, 128), ("x", 0): (4, 32), ("y", 1): (1, 32), ("x", 1): (1, 32)}
+    blocks, height = shapes[plan[2], stage]
+    return blocks, height, chunk_width(plan)
+
+
+def add_rows(blocks, height, reads, write):
     def one(step, carry):
-        block, row = step // (height // 16), lax.rem(step, height // 16) * 16
-        here = (
-            first_block + block,
-            pl.ds(pl.multiple_of(first_row + row, 16), 16),
-            pl.ds(first_column, width),
-        )
-        total = target[here].astype(jnp.float32)
-        for ref, base, column in sources:
-            total = total + ref[
-                base + block, pl.ds(pl.multiple_of(row, 16), 16), pl.ds(column, width)
-            ].astype(jnp.float32)
-        if dest is None:
-            target[here] = total.astype(jnp.bfloat16)
-        else:
-            dest[pl.ds(pl.multiple_of(row, 16), 16), pl.ds(first_column, width)] = total.astype(
-                jnp.bfloat16
-            )
+        block = step // (height // 16)
+        row = pl.multiple_of(lax.rem(step, height // 16) * 16, 16)
+        total = reads[0](block, row).astype(jnp.float32)
+        for read in reads[1:]:
+            total = total + read(block, row).astype(jnp.float32)
+        write(block, row, total.astype(jnp.bfloat16))
         return carry
 
     lax.fori_loop(0, blocks * (height // 16), one, 0)
 
 
-def reduce_kernel(parts, out, held, paired, final, crossed, *rest):
-    stage_refs, (send_sem, recv_sem, local_sem) = rest[:-3], rest[-3:]
+def reduce_kernel(*refs):
+    far, out = refs[:9], refs[9]
+    near, (staged, held, crossed, gathered) = refs[10:19], refs[19:23]
+    stage_refs, (load_sem, store_sem, send_sem, recv_sem) = refs[23:-4], refs[-4:]
+    rows_in, context, normed_low, activated, joined, first_low, pre_low, second_low, small = near
+    loads = [pltpu.make_async_copy(a, b, load_sem.at[n]) for n, (a, b) in enumerate(zip(far, near))]
+    needs = {0: (0, 4), 3: (1, 5), 4: (2, 6), 8: (3, 7), 12: (8,)}
+    sources = lambda unit: needs[max(key for key in needs if key <= unit)]
+    pending = []
+    for first, units, _ in REDUCE_PLAN:
+        for unit in (first, first + units - 1):
+            pending += [n for n in sources(unit) if n not in pending]
+    pending.append(8)
+    for n in pending:
+        loads[n].start()
     y, c, x, z = place()
     ring = {
         "y": (y, device(step_on(y, 1), c, x, z), device(step_on(y, -1), c, x, z)),
@@ -233,26 +241,56 @@
     partner = device(y, c, x, 1 - z)
     greet((ring["y"][1], ring["y"][2], ring["x"][1], ring["x"][2], sibling, partner))
     copies = Copies(send_sem, recv_sem)
-    own, from_sibling, from_here, offset = [], [], [], 0
-    offsets = []
-    for n, (part_a, part_b, _) in enumerate(REDUCE_PLAN):
-        width = (part_a + part_b) * TILE
-        columns = pl.ds(offset, width)
-        from_sibling.append(
-            copies.start(parts.at[:, 1 - c, :, columns], paired.at[:, :, columns], sibling)
-        )
-        local = pltpu.make_async_copy(
-            parts.at[:, c, :, columns], held.at[:, :, columns], local_sem.at[n]
-        )
-        local.start()
-        from_here.append(local)
-        offsets.append(offset)
-        offset += width
+    to_sibling, stores = [], []
+
+    def ready(numbers):
+        for n in numbers:
+            if n in pending:
+                loads[n].wait()
+                pending.remove(n)
+
+    def produce(n):
+        first, units, _ = REDUCE_PLAN[n]
+        slot = n % 2
+        for unit in range(first, first + units):
+            ready(sources(unit))
+
+        def block_rows(at, carry):
+            for unit in range(first, min(first + units, 8)):
+                if unit < 3:
+                    left, right, column = rows_in, joined, unit
+                elif unit == 3:
+                    left, right, column = context, first_low, 0
+                else:
+                    left, right, column = normed_low, pre_low, unit - 4
+                tile = dot_first(
+                    left[:, pl.ds(pl.multiple_of(at * 256, 256), 256)],
+                    right[:, column * WIDTH : (column + 1) * WIDTH],
+                ).astype(jnp.bfloat16)
+                place_at = slice((unit - first) * WIDTH, (unit - first + 1) * WIDTH)
+                staged[slot, at, :, :, place_at] = tile.reshape(2, TILE, WIDTH)
+            if first >= 8:
+                for core in (0, 1):
+                    start = at * WIDTH + core * 512 + (first - 8) * TILE
+                    rows = activated[:, pl.ds(pl.multiple_of(start, TILE), units * TILE)]
+                    tile = dot_first(rows, second_low[...]).astype(jnp.bfloat16)
+                    for unit in range(units):
+                        place_at = slice(unit * WIDTH, (unit + 1) * WIDTH)
+                        staged[slot, at, core, :, place_at] = tile[unit * TILE : (unit + 1) * TILE]
+            return carry
+
+        lax.fori_loop(0, 4, block_rows, 0)
+        if first + units == UNITS:
+            ready((8,))
+            for at in range(4):
+                for core in (0, 1):
+                    staged[slot, at, core, :, units * WIDTH : units * WIDTH + TILE] = small[at, core]
 
     def along(n, stage):
-        part_a, part_b, leading = REDUCE_PLAN[n]
-        wide_a, wide_b = part_a * TILE, part_b * TILE
-        start_a, start_b = offsets[n], offsets[n] + wide_a
+        first, _, leading = REDUCE_PLAN[n]
+        offset, wide_a = first * WIDTH, REDUCE_PLAN[n][1] * WIDTH // 2
+        wide_b = chunk_width(REDUCE_PLAN[n]) - wide_a
+        start_a, start_b = offset, offset + wide_a
         axis = leading if stage == 0 else ("x" if leading == "y" else "y")
         index, right, left = ring[axis]
         blocks, height, _ = stage_shape(REDUCE_PLAN[n], stage)
@@ -270,72 +308,121 @@
             ]
 
         def land(slot, start, wide):
-            return landing.at[pl.ds(slot * blocks, blocks), :, pl.ds(start - offsets[n], wide)]
+            return landing.at[pl.ds(slot * blocks, blocks), :, pl.ds(start - offset, wide)]
 
         def add(at, start, wide, slots):
-            block, row = origin(at)
-            add_into(
-                held,
-                (blocks, block, height, row),
-                (start, wide),
-                [(landing, slot * blocks, start - offsets[n]) for slot in slots],
-            )
+            first_block, first_row = origin(at)
+
+            def own(block, row):
+                return first_block + block, pl.ds(
+                    pl.multiple_of(first_row + row, 16), 16
+                ), pl.ds(start, wide)
+
+            def write(block, row, total):
+                held[own(block, row)] = total
+
+            def landed(slot):
+                return lambda block, row: landing[
+                    slot * blocks + block, pl.ds(row, 16), pl.ds(start - offset, wide)
+                ]
+
+            reads = [lambda block, row: held[own(block, row)], *[landed(slot) for slot in slots]]
+            add_rows(blocks, height, reads, write)
 
         ahead, behind, across = step_on(index, 1), step_on(index, -1), step_on(index, 2)
         far_right = copies.start(take(across, start_a, wide_a), land(0, start_a, wide_a), right)
         far_left = copies.start(take(across, start_b, wide_b), land(0, start_b, wide_b), left)
-        near = [
+        near_copies = [
             copies.start(take(ahead, start_b, wide_b), land(1, start_b, wide_b), right),
             copies.start(take(behind, start_a, wide_a), land(2, start_a, wide_a), left),
         ]
         yield
         far_right.wait_recv()
         add(ahead, start_a, wide_a, (0,))
-        near.append(copies.start(take(ahead, start_a, wide_a), land(1, start_a, wide_a), right))
+        near_copies.append(
+            copies.start(take(ahead, start_a, wide_a), land(1, start_a, wide_a), right)
+        )
         far_left.wait_recv()
         add(behind, start_b, wide_b, (0,))
-        near.append(copies.start(take(behind, start_b, wide_b), land(2, start_b, wide_b), left))
+        near_copies.append(
+            copies.start(take(behind, start_b, wide_b), land(2, start_b, wide_b), left)
+        )
         yield
-        for copy in near:
+        for copy in near_copies:
             copy.wait_recv()
         add(index, start_a, wide_a + wide_b, (1, 2))
 
     def chunk(n):
-        part_a, part_b, _ = REDUCE_PLAN[n]
-        start, wide_a, wide = offsets[n], part_a * TILE, (part_a + part_b) * TILE
+        plan = REDUCE_PLAN[n]
+        start, wide, slot = plan[0] * WIDTH, chunk_width(plan), n % 2
+        wide_a = plan[1] * WIDTH // 2
         columns = pl.ds(start, wide)
-        from_here[n].wait()
-        from_sibling[n].wait_recv()
-        add_into(held, (4, 0, 128, 0), (start, wide), [(paired, 0, start)])
+        if n >= 2:
+            copies.sent(to_sibling[n - 2])
+        produce(n)
+        to_sibling.append(
+            copies.start(
+                staged.at[slot, :, 1 - c, :, pl.ds(0, wide)], held.at[:, :, columns], sibling
+            )
+        )
+        yield
+        to_sibling[n].wait_recv()
+
+        def write(block, row, total):
+            held[block, pl.ds(row, 16), columns] = total
+
+        add_rows(
+            4,
+            128,
+            [
+                lambda block, row: held[block, pl.ds(row, 16), columns],
+                lambda block, row: staged[slot, block, c, pl.ds(row, 16), pl.ds(0, wide)],
+            ],
+            write,
+        )
         yield from along(n, 0)
         yield from along(n, 1)
-        rows = pl.ds(pl.multiple_of(x * 32, 16), 32)
-        swap = copies.start(held.at[pl.ds(y, 1), rows, columns], crossed.at[:, :, columns], partner)
+
+        def rows_of(at, first=start, width=wide):
+            return gathered.at[pl.ds(pl.multiple_of(at * 32, 16), 32), pl.ds(first, width)]
+
+        swap = copies.start(
+            held.at[pl.ds(y, 1), pl.ds(pl.multiple_of(x * 32, 16), 32), columns],
+            crossed.at[:, :, columns],
+            partner,
+        )
         yield
         swap.wait_recv()
-        add_into(held, (1, y, 32, x * 32), (start, wide), [(crossed, 0, start)], dest=final)
-        kept = pltpu.make_async_copy(
-            final.at[:, columns], out.at[rows, columns], local_sem.at[len(REDUCE_PLAN) + n]
+
+        def finish(block, row, total):
+            gathered[pl.ds(pl.multiple_of(x * 32 + row, 16), 16), columns] = total
+
+        add_rows(
+            1,
+            32,
+            [
+                lambda block, row: held[y, pl.ds(pl.multiple_of(x * 32 + row, 16), 16), columns],
+                lambda block, row: crossed[0, pl.ds(row, 16), columns],
+            ],
+            finish,
         )
-        kept.start()
-        own.append(kept)
         _, right, left = ring["x"]
-        to_right = copies.start(final.at[:, columns], out.at[rows, columns], right)
-        to_left = copies.start(final.at[:, columns], out.at[rows, columns], left)
+        to_right = copies.start(rows_of(x), rows_of(x), right)
+        to_left = copies.start(rows_of(x), rows_of(x), left)
         yield
         to_right.wait_recv()
-        block = out.at[
-            pl.ds(pl.multiple_of(step_on(x, -1) * 32, 16), 32), pl.ds(start, wide_a)
-        ]
+        block = rows_of(step_on(x, -1), start, wide_a)
         last = [copies.start(block, block, right)]
         to_left.wait_recv()
-        block = out.at[
-            pl.ds(pl.multiple_of(step_on(x, 1) * 32, 16), 32), pl.ds(start + wide_a, wide - wide_a)
-        ]
+        block = rows_of(step_on(x, 1), start + wide_a, wide - wide_a)
         last.append(copies.start(block, block, left))
         yield
         for copy in last:
             copy.wait_recv()
+        stores.append(
+            pltpu.make_async_copy(gathered.at[:, columns], out.at[:, columns], store_sem.at[n])
+        )
+        stores[-1].start()
 
     waiting = [chunk(n) for n in range(len(REDUCE_PLAN))]
     running = []
@@ -345,58 +432,74 @@
         for member in list(running):
             if next(member, "end") == "end":
                 running.remove(member)
-    for copy in own:
+    for copy in stores:
         copy.wait()
     copies.finish()
 
 
-def reduce_parts(parts):
+def reduce_grads(*operands):
     chunks = len(REDUCE_PLAN)
+    widest = max(chunk_width(plan) for plan in REDUCE_PLAN)
     landing = []
     for plan in REDUCE_PLAN:
         for stage in (0, 1):
             blocks, height, width = stage_shape(plan, stage)
             landing.append(pltpu.VMEM((3 * blocks, height, width), jnp.bfloat16))
+    far = pl.BlockSpec(memory_space=pl.ANY)
     return pl.pallas_call(
         reduce_kernel,
-        out_shape=jax.ShapeDtypeStruct((128, PAYLOAD), jnp.bfloat16),
-        in_specs=[pl.BlockSpec(memory_space=pl.ANY)],
-        out_specs=pl.BlockSpec(memory_space=pl.ANY),
+        out_shape=jax.ShapeDtypeStruct((TILE, PAYLOAD), jnp.bfloat16),
+        in_specs=[far] * len(operands),
+        out_specs=far,
         scratch_shapes=[
-            pltpu.VMEM((4, 128, PAYLOAD), jnp.bfloat16),
-            pltpu.VMEM((4, 128, PAYLOAD), jnp.bfloat16),
-            pltpu.VMEM((32, PAYLOAD), jnp.bfloat16),
+            *[pltpu.VMEM(operand.shape, operand.dtype) for operand in operands],
+            pltpu.VMEM((2, 4, 2, TILE, widest), jnp.bfloat16),
+            pltpu.VMEM((4, TILE, PAYLOAD), jnp.bfloat16),
             pltpu.VMEM((1, 32, PAYLOAD), jnp.bfloat16),
+            pltpu.VMEM((TILE, PAYLOAD), jnp.bfloat16),
             *landing,
+            pltpu.SemaphoreType.DMA((len(operands),)),
+            pltpu.SemaphoreType.DMA((chunks,)),
             pltpu.SemaphoreType.DMA((chunks * 18,)),
             pltpu.SemaphoreType.DMA((chunks * 18,)),
-            pltpu.SemaphoreType.DMA((chunks * 2,)),
         ],
         compiler_params=pltpu.CompilerParams(
             collective_id=1, has_side_effects=True, vmem_limit_bytes=VMEM_CAP
         ),
-        name="reduce_parts",
-    )(parts)
-
-
-EPSILON = 1e-05
-ROWS = 256
-WIDTH = 1024
-FF_WIDTH = 4096
-STRIP = 32
-FF_STEP = 512
-
-
-def dot(a, b):
-    return jnp.dot(a, b, preferred_element_type=jnp.float32)
-
-
-def dot_last(a, b):
-    return lax.dot_general(a, b, (((1,), (1,)), ((), ())), preferred_element_type=jnp.float32)
-
-
-def dot_first(a, b):
-    return lax.dot_general(a, b, (((0,), (0,)), ((), ())), preferred_element_type=jnp.float32)
+        name="reduce_grads",
+    )(*operands)
+
+
+def widen_kernel(low, qkv, out, into, down, bias, gain, hidden):
+    total = low[...].astype(jnp.float32)
+    qkv[...] = total[:, :3072]
+    out[...] = total[:, 3072:4096]
+    into[...] = total[:, 4096:8192]
+    for j in range(4):
+        down[j] = total[:, 8192 + j * WIDTH : 8192 + (j + 1) * WIDTH]
+
+    @pl.when(pl.program_id(0) == 0)
+    def _():
+        bias[...] = total[0:6, 12288:]
+        gain[...] = total[6:8, 12288:]
+        hidden[...] = total[8:12, 12288:]
+
+
+def widen_outputs(total):
+    step = 32
+    shapes = [(TILE, 3072), (TILE, WIDTH), (TILE, 4096), (4, TILE, WIDTH), (6, TILE), (2, TILE), (4, TILE)]
+    specs = [pl.BlockSpec((step, shape[1]), lambda i: (i, 0)) for shape in shapes[:3]]
+    specs.append(pl.BlockSpec((4, step, WIDTH), lambda i: (0, i, 0)))
+    specs += [pl.BlockSpec(shape, lambda i: (0, 0)) for shape in shapes[4:]]
+    outs = pl.pallas_call(
+        widen_kernel,
+        grid=(TILE // step,),
+        out_shape=[jax.ShapeDtypeStruct(shape, jnp.float32) for shape in shapes],
+        in_specs=[pl.BlockSpec((step, PAYLOAD), lambda i: (i, 0))],
+        out_specs=specs,
+        name="widen_outputs",
+    )(total)
+    return (*outs[:3], outs[3].reshape(512, WIDTH), outs[4], outs[5], outs[6].reshape(512))
 
 
 def row_mean(rows):
@@ -426,17 +529,26 @@
     ends,
     id_column,
     id_row,
-    w_qkv_far,
-    w_out_far,
-    w_in_far,
-    w_down_far,
-    small,
+    w_qkv_shard,
+    w_out_shard,
+    w_in_shard,
+    w_down_shard,
+    small_shard,
     ends_out,
-    parts,
+    rows_in_far,
+    context_far,
+    normed_low_far,
+    activated_far,
+    joined_far,
+    first_low_far,
+    pre_low_far,
+    second_low_far,
+    small_far,
     w_qkv,
     w_out,
     w_in,
     w_down,
+    small,
     vec,
     sums,
     rows_in,
@@ -458,25 +570,32 @@
     first_low,
     joined,
     total,
-    tiles,
     small_rows,
     small_tile,
     load_sem,
     store_sem,
     send_sem,
     recv_sem,
+    gather_send_sem,
+    gather_recv_sem,
 ):
     section = lax.axis_index("section")
-    loads = [
-        pltpu.make_async_copy(far, near, load_sem.at[n])
-        for n, (far, near) in enumerate(
-            ((w_qkv_far, w_qkv), (w_out_far, w_out), (w_in_far, w_in), (w_down_far, w_down))
-        )
-    ]
-    for load in loads:
-        load.start()
     other = {"section": 1 - section}
-    greet((other,))
+    copies = Copies(gather_send_sem, gather_recv_sem)
+    arrived = gather_into(
+        (w_qkv_shard, w_out_shard, w_in_shard, w_down_shard, small_shard),
+        (w_qkv, w_out, w_in, w_down, small),
+        copies,
+        load_sem,
+        (other,),
+    )
+    stores = []
+
+    def store(near, far):
+        copy = pltpu.make_async_copy(near, far, store_sem.at[len(stores)])
+        copy.start()
+        stores.append(copy)
+
     onward = pltpu.make_async_remote_copy(
         src_ref=leaving, dst_ref=rows_in, send_sem=send_sem.at[0], recv_sem=recv_sem.at[0],
         device_id=other, device_id_type=MESH,
@@ -485,6 +604,7 @@
         src_ref=leaving, dst_ref=cotangent, send_sem=send_sem.at[1], recv_sem=recv_sem.at[1],
         device_id=other, device_id_type=MESH,
     )
+    arrived(4)
     for f in range(N_F):
         shard = small[f * SMALL_ROWS : (f + 1) * SMALL_ROWS, :TILE].astype(jnp.float32)
         vec[0:8, f * TILE : (f + 1) * TILE] = shard[0:8]
@@ -506,7 +626,8 @@
         cotangent[...] = ends[...]
         onward.wait_recv()
 
-    loads[0].wait()
+    arrived(0)
+    store(rows_in, rows_in_far)
     for j in range(6):
         columns = slice(j * 512, (j + 1) * 512)
         projected = dot(rows_in[...], w_qkv[:, columns])
@@ -540,7 +661,8 @@
         return carry
 
     lax.fori_loop(0, HEADS // 2, attend, 0)
-    loads[1].wait()
+    arrived(1)
+    store(context, context_far)
     total[...] = dot(context[...], w_out[...])
 
     def first_norm(rows):
@@ -553,8 +675,9 @@
         normed_low[rows, :] = shifted.astype(jnp.bfloat16)
 
     strips(first_norm)
-    loads[2].wait()
-    loads[3].wait()
+    store(normed_low, normed_low_far)
+    arrived(2)
+    arrived(3)
 
     def widen(j):
         columns = slice(j * FF_STEP, (j + 1) * FF_STEP)
@@ -572,6 +695,8 @@
         columns = slice(n * 512, (n + 1) * 512)
         total[:, columns] = dot(activated[...], w_down[:, columns])
 
+    store(activated, activated_far)
+
     def second_norm(rows):
         summed = normed_out[rows, :] + total[rows, :] + vec[4:5, :]
         normed, inverse = norm_forward(summed)
@@ -605,6 +730,7 @@
         second_low[rows, :] = grad.astype(jnp.bfloat16)
 
     strips(second_back)
+    store(second_low, second_low_far)
     for j in range(FF_WIDTH // FF_STEP):
         columns = slice(j * FF_STEP, (j + 1) * FF_STEP)
         row, first = j * FF_STEP // WIDTH, j * FF_STEP % WIDTH
@@ -615,6 +741,8 @@
         columns = slice(n * 512, (n + 1) * 512)
         total[:, columns] = dot_last(pre_low[...], w_in[columns, :])
 
+    store(pre_low, pre_low_far)
+
     def first_back(rows):
         grad = normed_out[rows, :] + total[rows, :]
         normed = first_normed[rows, :]
@@ -626,6 +754,7 @@
         first_low[rows, :] = grad.astype(jnp.bfloat16)
 
     strips(first_back)
+    store(first_low, first_low_far)
     context_grad = leaving
     for n in range(2):
         columns = slice(n * 512, (n + 1) * 512)
@@ -657,6 +786,7 @@
         return carry
 
     lax.fori_loop(0, HEADS // 2, attend_back, 0)
+    store(joined, joined_far)
     for n in range(2):
         columns = slice(n * 512, (n + 1) * 512)
         grad = normed_out[:, columns] + dot_last(joined[...], w_qkv[columns, :])
@@ -679,64 +809,24 @@
     small_tile[...] = jnp.zeros_like(small_tile)
     for f in range(N_F):
         small_tile[f // 2, f % 2, 0:16, :] = small_rows[f].astype(jnp.bfloat16)
-    small_copy = pltpu.make_async_copy(
-        small_tile, parts.at[:, :, :, 12 * WIDTH : 12 * WIDTH + TILE], store_sem.at[12]
-    )
-    small_copy.start()
-
-    def store(slot, y):
-        return pltpu.make_async_copy(
-            tiles.at[slot],
-            parts.at[y, :, :, slot * WIDTH : (slot + 1) * WIDTH],
-            store_sem.at[slot],
-        )
-
-    def weight_grads(y, carry):
-        block = pl.ds(pl.multiple_of(y * 256, 256), 256)
-
-        @pl.when(y > 0)
-        def _():
-            for slot in range(12):
-                store(slot, y - 1).wait()
-
-        for slot in range(8):
-            if slot < 3:
-                left, right, column = rows_in, joined, slot
-            elif slot == 3:
-                left, right, column = context, first_low, 0
-            else:
-                left, right, column = normed_low, pre_low, slot - 4
-            tile = dot_first(left[:, block], right[:, column * WIDTH : (column + 1) * WIDTH])
-            tiles[slot] = tile.astype(jnp.bfloat16).reshape(2, TILE, WIDTH)
-            store(slot, y).start()
-        for core in (0, 1):
-            for pair in (0, 1):
-                first = pl.multiple_of(y * WIDTH + core * 512 + pair * 256, 256)
-                tile = dot_first(activated[:, pl.ds(first, 256)], second_low[...])
-                low = tile.astype(jnp.bfloat16)
-                tiles[8 + 2 * pair, core] = low[:TILE]
-                tiles[9 + 2 * pair, core] = low[TILE:]
-        for slot in range(8, 12):
-            store(slot, y).start()
-        return carry
-
-    lax.fori_loop(0, 4, weight_grads, 0)
-    for slot in range(12):
-        store(slot, 3).wait()
-    small_copy.wait()
+    store(small_tile, small_far)
+    for copy in stores:
+        copy.wait()
+    copies.finish()
 
     @pl.when(section == 1)
     def _():
         back.wait_send()
 
 
-def run_layer(ends, ids, weights, small):
+def run_layer(ends, ids, shards):
     low, full = jnp.bfloat16, jnp.float32
     scratch = [
         ((1024, 3072), low),
         ((1024, 1024), low),
         ((1024, 4096), low),
         ((4096, 1024), low),
+        ((N_F * SMALL_ROWS, 2 * TILE), low),
         ((16, WIDTH), full),
         ((16, WIDTH), full),
         ((ROWS, WIDTH), low),
@@ -758,7 +848,6 @@
         ((ROWS, WIDTH), low),
         ((ROWS, 3 * WIDTH), low),
         ((ROWS, WIDTH), full),
-        ((12, 2, TILE, WIDTH), low),
         ((N_F, SMALL_ROWS, TILE), full),
         ((4, 2, TILE, TILE), low),
     ]
@@ -768,22 +857,25 @@
         layer_kernel,
         out_shape=[
             jax.ShapeDtypeStruct((ROWS, WIDTH), low),
-            jax.ShapeDtypeStruct((4, 2, TILE, PAYLOAD), low),
+            *[jax.ShapeDtypeStruct((ROWS, columns * WIDTH), low) for columns in (1, 1, 1, 4, 3, 1, 4, 1)],
+            jax.ShapeDtypeStruct((4, 2, TILE, TILE), low),
         ],
-        in_specs=[near, near, near, far, far, far, far, near],
-        out_specs=[near, far],
+        in_specs=[near, near, near, far, far, far, far, far],
+        out_specs=[near, *[far] * 9],
         scratch_shapes=[
             *[pltpu.VMEM(shape, kind) for shape, kind in scratch],
-            pltpu.SemaphoreType.DMA((4,)),
-            pltpu.SemaphoreType.DMA((13,)),
+            pltpu.SemaphoreType.DMA((5,)),
+            pltpu.SemaphoreType.DMA((9,)),
             pltpu.SemaphoreType.DMA((2,)),
             pltpu.SemaphoreType.DMA((2,)),
+            pltpu.SemaphoreType.DMA((GATHER_COPIES,)),
+            pltpu.SemaphoreType.DMA((GATHER_COPIES,)),
         ],
         compiler_params=pltpu.CompilerParams(
             collective_id=2, has_side_effects=True, vmem_limit_bytes=VMEM_CAP
         ),
         name="run_layer",
-    )(ends, ids[:, None], ids[None, :], *weights, small)
+    )(ends, ids[:, None], ids[None, :], *shards)
 
 
 def pack_small(biases, gains, bias_in):
@@ -791,27 +883,12 @@
     return jnp.pad(rows, ((0, 4), (0, TILE)))
 
 
-def split_total(total):
-    small = total[:, 12288:]
-    return (
-        total[:, :3072],
-        total[:, 3072:4096],
-        total[:, 4096:8192],
-        jnp.swapaxes(total[:, 8192:12288].reshape(TILE, 4, 1024), 0, 1).reshape(512, 1024),
-        small[:6],
-        small[6:8],
-        small[8:12].reshape(512),
-    )
-
-
 def body(ends_in, segment_ids, w_qkv, w_out, w_in, w_down, biases, gains, bias_in):
-    gathered = gather_weights(
-        w_qkv[0], w_out[0], w_in[0], w_down[0], pack_small(biases[0], gains[0], bias_in[0])
-    )
+    shards = (w_qkv[0], w_out[0], w_in[0], w_down[0], pack_small(biases[0], gains[0], bias_in[0]))
     ids = segment_ids + (lax.iota(jnp.int32, ROWS) // SEQ) * 16
-    ends_out, parts = run_layer(ends_in[0], ids, gathered[:4], gathered[4])
-    total = reduce_parts(parts).astype(jnp.float32)
-    return tuple(member[None] for member in (ends_out, *split_total(total)))
+    ends_out, *operands = run_layer(ends_in[0], ids, shards)
+    outs = widen_outputs(reduce_grads(*operands))
+    return tuple(member[None] for member in (ends_out, *outs))
 
 
 def solution(mesh):

time: 351 us -> 306 us (0.87)
  local copies, waits for them, and re-layouts: 34 us -> 2.87 us
  Pallas kernels: 312 us -> 299 us
    pallas_call x2, Pallas kernels: 198 us -> 127 us  [the longest x1 122 us: reduce_grads(): pl.pallas_call(reduce_kernel, out_shape=jax.ShapeDtypeStruct((TILE, PAYLO...]
    pallas_call x1, Pallas kernels: 113 us -> 172 us  [run_layer(): pl.pallas_call(layer_kernel, out_shape=[jax.ShapeDtypeStruct((ROWS, WIDTH...]
    unnamed x26 -> x6, local copies, waits for them, and re-layouts: 17 us -> 2.07 us
    broadcast_in_dim x5 -> x0, local copies, waits for them, and re-layouts: 4.26 us -> none  [body(): return tuple((member[None] for member in (ends_out, *split_total(total))))]
    slice x2 -> x0, local copies, waits for them, and re-layouts: 4.16 us -> none  [the longest x1 2.91 us: split_total(): total[:, 8192:12288].reshape(TILE, 4, 1024)]
    transpose x1 -> x0, local copies, waits for them, and re-layouts: 4.13 us -> none  [split_total(): jnp.swapaxes(total[:, 8192:12288].reshape(TILE, 4, 1024), 0, 1)]
    reshape x1 -> x0, local copies, waits for them, and re-layouts: 3.62 us -> none  [split_total(): total[:, 8192:12288].reshape(TILE, 4, 1024)]
where the time goes in v3:
time: 306 us; the launch traced here: 305 us
  Pallas kernels  299 us (98%)
    pallas_call x1, Pallas kernels, run_layer(): pl.pallas_call(layer_kernel, out_shape=[jax.ShapeDtypeStruct((ROWS, WIDTH...  172 us
    pallas_call x1, Pallas kernels, reduce_grads(): pl.pallas_call(reduce_kernel, out_shape=jax.ShapeDtypeStruct((TILE, PAYLO...  122 us

profile of v3, /device:TPU:6, one launch (start us, length us, event | category | flops | bytes accessed | tf_op | source)
XLA Modules:
  0.0 305.2 jit_solution(6270814925147561898)
XLA Ops:
  0.6 0.7 fusion.10
  1.3 0.0 copy-start.1
  1.3 0.7 reduce
  2.0 1.3 fusion.8.small_shard
  3.3 0.8 copy.18.id_column
  4.1 0.0 copy-done.1
  4.1 172.3 %run_layer.1 = (bf16[256,1024]{1,0:T(8,128)(2,1)}, bf16[256,1024]{1,0:T(8,128)(2,1)}, bf16[256,1024]{1,0:T(8,128)(2,1)}, bf16[256,1024]{1,0:T(8,128)(2,1)}, bf16...) custom-call(bf16[256,1024]{1,0:T(8,128)(2,1)} %bitcast.22, ...), custom_call_target="tpu_custom_call" | custom-call | tf_op jit(solution)/shard_map/run_layer/pallas_call | solution.py:856
  176.5 121.5 %reduce_grads.1.low = bf16[128,12416]{1,0:T(8,128)(2,1)} custom-call(bf16[256,1024]{1,0:T(8,128)(2,1)} %get-tuple-element.26.refs_0_, bf16[256,1024]{1,0:T(8,128)(2,1)} %get-tuple-element.27.refs_1_, bf16[256,1024]{1,0:T(8,128)(2,1)} %get-tuple-element.28.refs_2_, bf16[256,4096]{1,0:T(8,128)(2,1)} %get-tuple-element.29.refs_3_, ...), custom_call_target="tpu_custom_call" | custom-call | tf_op jit(solution)/shard_map/reduce_grads/pallas_call | solution.py:449
  298.0 0.0 copy-start
  298.0 5.1 %widen_outputs.1 = (f32[128,3072]{1,0:T(8,128)}, f32[128,1024]{1,0:T(8,128)}, f32[128,4096]{1,0:T(8,128)}, f32[4,128,1024]{2,1,0:T(8,128)}, f32[6,128]{1,0:T(8,1...) custom-call(bf16[128,12416]{1,0:T(8,128)(2,1)} %reduce_grads.1.low), custom_call_target="tpu_custom_call" | custom-call | tf_op jit(solution)/shard_map/widen_outputs/pallas_call | solution.py:494
  303.1 1.3 copy.19
  304.4 0.0 copy-done
  304.4 0.8 copy.21
Async XLA Ops:
  1.3 2.8 copy-start.1
  298.0 6.4 %copy-start = (bf16[256,1024]{1,0:T(8,128)(2,1)S(1)}, bf16[256,1024]{1,0:T(8,128)(2,1)}, u32[]{:S(2)}) copy-start(bf16[256,1024]{1,0:T(8,128)(2,1)} %get-tuple-element.25) | copy-start | bytes 1572868

commit v4 on v3

--- a/solution.py
+++ b/solution.py
@@ -114,63 +114,66 @@
 
     relayed = [k for k in range(count) if GATHER_PLAN[k][2]]
     direct = [k for k in range(count) if GATHER_PLAN[k][0] > 4 * GATHER_PLAN[k][2]]
-    first_right, first_left, loaded = {}, {}, []
-    for kind, members in (("relay", relayed), ("direct", direct)):
-        for k in members:
-            shard_rows, _, piece = GATHER_PLAN[k]
-            if kind == "relay":
-                first, rows = quarter(k, x), piece
-            else:
-                first, rows = 4 * piece, shard_rows - 4 * piece
-            if k not in loaded:
-                own[k].wait()
-                loaded.append(k)
-            src = span(k, y, first, rows)
-            first_right[kind, k] = copies.start(src, src, right_y)
-            first_left[kind, k] = copies.start(src, src, left_y)
-    sibling_copies = {}
+    first_right, first_left, second_right, second_left = {}, {}, {}, {}
+    along_right, along_left, sibling_copies, further = {}, {}, {}, {}
+    before, after, across = owners = (step_on(y, -1), step_on(y, 1), step_on(y, 2))
+
+    def extent(kind, k):
+        shard_rows, _, piece = GATHER_PLAN[k]
+        return (quarter(k, x), piece) if kind == "relay" else (4 * piece, shard_rows - 4 * piece)
+
+    def send_own(kind, k):
+        block = span(k, y, *extent(kind, k))
+        first_right[kind, k] = copies.start(block, block, right_y)
+        first_left[kind, k] = copies.start(block, block, left_y)
+
+    def send_on(kind, k):
+        first_right[kind, k].wait_recv()
+        block = span(k, before, *extent(kind, k), 0)
+        second_right[kind, k] = copies.start(block, block, right_y)
+        first_left[kind, k].wait_recv()
+        block = span(k, after, *extent(kind, k), 1)
+        second_left[kind, k] = copies.start(block, block, left_y)
+
+    def send_along(n, k):
+        block = span(k, owners[n], *extent("relay", k))
+        along_right[n, k] = copies.start(block, block, right_x)
+        along_left[n, k] = copies.start(block, block, left_x)
+
+    def send_further(n, k):
+        piece = GATHER_PLAN[k][2]
+        along_right[n, k].wait_recv()
+        block = span(k, owners[n], quarter(k, step_on(x, -1)), piece, 0)
+        further[n, k, 0] = copies.start(block, block, right_x)
+        along_left[n, k].wait_recv()
+        block = span(k, owners[n], quarter(k, step_on(x, 1)), piece, 1)
+        further[n, k, 1] = copies.start(block, block, left_x)
+
+    for k in relayed:
+        own[k].wait()
+        send_own("relay", k)
     for k in range(count):
+        if k not in relayed:
+            own[k].wait()
         block = span(k, y, 0, GATHER_PLAN[k][0])
         sibling_copies[3, k] = copies.start(block, block, sibling)
-
-    before, after, across = step_on(y, -1), step_on(y, 1), step_on(y, 2)
-    second_right, second_left = {}, {}
-    along_right, along_left = {}, {}
-    for kind, members in (("relay", relayed), ("direct", direct)):
-        for k in members:
-            shard_rows, _, piece = GATHER_PLAN[k]
-            if kind == "relay":
-                first, rows = quarter(k, x), piece
-            else:
-                first, rows = 4 * piece, shard_rows - 4 * piece
-            first_right[kind, k].wait_recv()
-            block = span(k, before, first, rows, 0)
-            second_right[kind, k] = copies.start(block, block, right_y)
-            first_left[kind, k].wait_recv()
-            block = span(k, after, first, rows, 1)
-            second_left[kind, k] = copies.start(block, block, left_y)
-            if kind == "relay":
-                for n, owner in ((0, before), (1, after)):
-                    block = span(k, owner, first, rows)
-                    along_right[n, k] = copies.start(block, block, right_x)
-                    along_left[n, k] = copies.start(block, block, left_x)
+    for k in relayed:
+        send_on("relay", k)
+        send_along(0, k)
+        send_along(1, k)
+    for k in direct[::-1]:
+        send_own("direct", k)
     for k in relayed:
         second_right["relay", k].wait_recv()
         second_left["relay", k].wait_recv()
-        block = span(k, across, quarter(k, x), GATHER_PLAN[k][2])
-        along_right[2, k] = copies.start(block, block, right_x)
-        along_left[2, k] = copies.start(block, block, left_x)
-    further = {}
-    owners = (before, after, across)
-    for n in range(3):
+        send_along(2, k)
+    for n in (0, 1):
         for k in relayed:
-            piece = GATHER_PLAN[k][2]
-            along_right[n, k].wait_recv()
-            block = span(k, owners[n], quarter(k, step_on(x, -1)), piece, 0)
-            further[n, k, 0] = copies.start(block, block, right_x)
-            along_left[n, k].wait_recv()
-            block = span(k, owners[n], quarter(k, step_on(x, 1)), piece, 1)
-            further[n, k, 1] = copies.start(block, block, left_x)
+            send_further(n, k)
+    for k in direct[::-1]:
+        send_on("direct", k)
+    for k in relayed:
+        send_further(2, k)
     for k in range(count):
         for n in range(3):
             if n == 2 and k in direct:
@@ -189,7 +192,9 @@
     return arrived
 
 
-REDUCE_PLAN = ((4, 2, "y"), (6, 2, "x"), (0, 2, "y"), (2, 2, "y"), (8, 2, "x"), (10, 2, "y"))
+REDUCE_PLAN = tuple(
+    (unit, 1, "yxy"[n % 3]) for n, unit in enumerate((4, 5, 6, 7, 0, 1, 2, 3, 8, 9, 10, 11))
+)
 UNITS = 12
 
 
@@ -429,7 +434,7 @@
     while waiting or running:
         if waiting:
             running.append(waiting.pop(0))
-        for member in list(running):
+        for member in running[::-1]:
             if next(member, "end") == "end":
                 running.remove(member)
     for copy in stores:

time: 306 us -> 290 us (0.948)
  Pallas kernels: 299 us -> 284 us
    pallas_call x1, Pallas kernels: 122 us -> 112 us  [reduce_grads(): pl.pallas_call(reduce_kernel, out_shape=jax.ShapeDtypeStruct((TILE, PAYLO...]
    pallas_call x1, Pallas kernels: 172 us -> 166 us  [run_layer(): pl.pallas_call(layer_kernel, out_shape=[jax.ShapeDtypeStruct((ROWS, WIDTH...]
where the time goes in v4:
time: 290 us
  Pallas kernels  284 us (98%)
    pallas_call x1, Pallas kernels, run_layer(): pl.pallas_call(layer_kernel, out_shape=[jax.ShapeDtypeStruct((ROWS, WIDTH...  166 us
    pallas_call x1, Pallas kernels, reduce_grads(): pl.pallas_call(reduce_kernel, out_shape=jax.ShapeDtypeStruct((TILE, PAYLO...  112 us

profile of v4, /device:TPU:6, one launch (start us, length us, event | category | flops | bytes accessed | tf_op | source)
XLA Modules:
  0.0 289.9 jit_solution(17775559024204553636)
XLA Ops:
  0.6 0.7 fusion.10
  1.3 0.0 copy-start.1
  1.3 0.7 reduce
  2.0 1.3 fusion.8.small_shard
  3.3 0.8 copy.18.id_column
  4.1 0.0 copy-done.1
  4.1 166.4 %run_layer.1 = (bf16[256,1024]{1,0:T(8,128)(2,1)}, bf16[256,1024]{1,0:T(8,128)(2,1)}, bf16[256,1024]{1,0:T(8,128)(2,1)}, bf16[256,1024]{1,0:T(8,128)(2,1)}, bf16...) custom-call(bf16[256,1024]{1,0:T(8,128)(2,1)} %bitcast.22, ...), custom_call_target="tpu_custom_call" | custom-call | tf_op jit(solution)/shard_map/run_layer/pallas_call | solution.py:861
  170.5 112.1 %reduce_grads.1.low = bf16[128,12416]{1,0:T(8,128)(2,1)} custom-call(bf16[256,1024]{1,0:T(8,128)(2,1)} %get-tuple-element.26.refs_0_, bf16[256,1024]{1,0:T(8,128)(2,1)} %get-tuple-element.27.refs_1_, bf16[256,1024]{1,0:T(8,128)(2,1)} %get-tuple-element.28.refs_2_, bf16[256,4096]{1,0:T(8,128)(2,1)} %get-tuple-element.29.refs_3_, ...), custom_call_target="tpu_custom_call" | custom-call | tf_op jit(solution)/shard_map/reduce_grads/pallas_call | solution.py:454
  282.7 0.0 copy-start
  282.7 5.1 %widen_outputs.1 = (f32[128,3072]{1,0:T(8,128)}, f32[128,1024]{1,0:T(8,128)}, f32[128,4096]{1,0:T(8,128)}, f32[4,128,1024]{2,1,0:T(8,128)}, f32[6,128]{1,0:T(8,1...) custom-call(bf16[128,12416]{1,0:T(8,128)(2,1)} %reduce_grads.1.low), custom_call_target="tpu_custom_call" | custom-call | tf_op jit(solution)/shard_map/widen_outputs/pallas_call | solution.py:499
  287.8 1.3 copy.19
  289.1 0.0 copy-done
  289.1 0.8 copy.21
Async XLA Ops:
  1.3 2.8 copy-start.1
  282.7 6.4 %copy-start = (bf16[256,1024]{1,0:T(8,128)(2,1)S(1)}, bf16[256,1024]{1,0:T(8,128)(2,1)}, u32[]{:S(2)}) copy-start(bf16[256,1024]{1,0:T(8,128)(2,1)} %get-tuple-element.25) | copy-start | bytes 1572868

commit v5 on v4

--- a/solution.py
+++ b/solution.py
@@ -13,6 +13,7 @@
 WIDTH = 1024
 FF_WIDTH = 4096
 STRIP = 32
+HALF = 128
 FF_STEP = 512
 
 
@@ -522,12 +523,20 @@
     return inverse * (scaled - row_mean(scaled) - normed * row_mean(scaled * normed))
 
 
-def strips(body):
+def strips(body, first):
     def one(n, carry):
-        body(pl.ds(pl.multiple_of(n * STRIP, STRIP), STRIP))
+        body(pl.ds(pl.multiple_of(first + n * STRIP, STRIP), STRIP))
         return carry
 
-    lax.fori_loop(0, ROWS // STRIP, one, 0)
+    lax.fori_loop(0, HALF // STRIP, one, 0)
+
+
+def halves(body):
+    def one(n, carry):
+        body(n, pl.multiple_of(n * HALF, HALF))
+        return carry
+
+    lax.fori_loop(0, 2, one, 0)
 
 
 def layer_kernel(
@@ -601,14 +610,17 @@
         copy.start()
         stores.append(copy)
 
-    onward = pltpu.make_async_remote_copy(
-        src_ref=leaving, dst_ref=rows_in, send_sem=send_sem.at[0], recv_sem=recv_sem.at[0],
-        device_id=other, device_id_type=MESH,
-    )
-    back = pltpu.make_async_remote_copy(
-        src_ref=leaving, dst_ref=cotangent, send_sem=send_sem.at[1], recv_sem=recv_sem.at[1],
-        device_id=other, device_id_type=MESH,
-    )
+    def passing(first, landing, number):
+        rows = pl.ds(first, HALF)
+        return pltpu.make_async_remote_copy(
+            src_ref=leaving.at[rows, :],
+            dst_ref=landing.at[rows, :],
+            send_sem=send_sem.at[number],
+            recv_sem=recv_sem.at[number],
+            device_id=other,
+            device_id_type=MESH,
+        )
+
     arrived(4)
     for f in range(N_F):
         shard = small[f * SMALL_ROWS : (f + 1) * SMALL_ROWS, :TILE].astype(jnp.float32)
@@ -629,25 +641,29 @@
     @pl.when(section == 1)
     def _():
         cotangent[...] = ends[...]
-        onward.wait_recv()
-
-    arrived(0)
-    store(rows_in, rows_in_far)
-    for j in range(6):
-        columns = slice(j * 512, (j + 1) * 512)
-        projected = dot(rows_in[...], w_qkv[:, columns])
-        if j // 2 != 1:
-            row = 0 if j < 2 else 1
-            first = (j % 2) * 512
-            projected = projected + vec[row : row + 1, first : first + 512]
-        qkv[:, columns] = projected.astype(jnp.bfloat16)
-
+
+    for k in range(4):
+        arrived(k)
     def head_columns(p, part):
         return pl.ds(pl.multiple_of(part * WIDTH + p * TILE, TILE), TILE)
 
-    def attend(p, carry):
-        for b in (0, 1):
-            rows = slice(b * TILE, (b + 1) * TILE)
+    def forward(number, first_row):
+        rows = pl.ds(first_row, HALF)
+
+        @pl.when(section == 1)
+        def _():
+            passing(first_row, rows_in, number).wait_recv()
+
+        for j in range(6):
+            columns = slice(j * 512, (j + 1) * 512)
+            projected = dot(rows_in[rows, :], w_qkv[:, columns])
+            if j // 2 != 1:
+                row = 0 if j < 2 else 1
+                first = (j % 2) * 512
+                projected = projected + vec[row : row + 1, first : first + 512]
+            qkv[rows, columns] = projected.astype(jnp.bfloat16)
+
+        def attend(p, carry):
             query = qkv[rows, head_columns(p, 0)]
             key = qkv[rows, head_columns(p, 1)]
             value = qkv[rows, head_columns(p, 2)]
@@ -659,115 +675,120 @@
                 exponent = jnp.exp(scores - jnp.max(scores, axis=-1, keepdims=True))
                 share = exponent / jnp.sum(exponent, axis=-1, keepdims=True)
                 low = share.astype(jnp.bfloat16)
-                chances[p * 4 + b * 2 + h] = low
+                chances[p * 4 + number * 2 + h] = low
                 part = dot(low, value * head_masks[h])
                 mixed = part if mixed is None else mixed + part
             context[rows, head_columns(p, 0)] = mixed.astype(jnp.bfloat16)
-        return carry
-
-    lax.fori_loop(0, HEADS // 2, attend, 0)
-    arrived(1)
+            return carry
+
+        lax.fori_loop(0, HEADS // 2, attend, 0)
+        total[rows, :] = dot(context[rows, :], w_out[...])
+
+        def first_norm(rows):
+            summed = rows_in[rows, :].astype(jnp.float32) + total[rows, :] + vec[2:3, :]
+            normed, inverse = norm_forward(summed)
+            first_normed[rows, :] = normed
+            first_inverse[rows, :] = jnp.broadcast_to(inverse, (STRIP, TILE))
+            shifted = normed * vec[6:7, :] + vec[3:4, :]
+            normed_out[rows, :] = shifted
+            normed_low[rows, :] = shifted.astype(jnp.bfloat16)
+
+        strips(first_norm, first_row)
+
+        def widen(j):
+            columns = slice(j * FF_STEP, (j + 1) * FF_STEP)
+            row, first = j * FF_STEP // WIDTH, j * FF_STEP % WIDTH
+            pre_act = dot(normed_low[rows, :], w_in[:, columns])
+            pre_act = pre_act + vec[8 + row : 9 + row, first : first + FF_STEP]
+            phi = 0.5 * (1.0 + lax.erf(pre_act * 0.7071067811865476))
+            activated[rows, columns] = (pre_act * phi).astype(jnp.bfloat16)
+            density = jnp.exp(-0.5 * pre_act * pre_act) * 0.3989422804014327
+            slope[rows, columns] = (phi + pre_act * density).astype(jnp.bfloat16)
+
+        for j in range(FF_WIDTH // FF_STEP):
+            widen(j)
+        for n in range(2):
+            columns = slice(n * 512, (n + 1) * 512)
+            total[rows, columns] = dot(activated[rows, :], w_down[:, columns])
+
+
+        def second_norm(rows):
+            summed = normed_out[rows, :] + total[rows, :] + vec[4:5, :]
+            normed, inverse = norm_forward(summed)
+            second_normed[rows, :] = normed
+            second_inverse[rows, :] = jnp.broadcast_to(inverse, (STRIP, TILE))
+            leaving[rows, :] = (normed * vec[7:8, :] + vec[5:6, :]).astype(jnp.bfloat16)
+
+        strips(second_norm, first_row)
+
+        @pl.when(section == 0)
+        def _():
+            passing(first_row, rows_in, number).start()
+
+        @pl.when(section == 1)
+        def _():
+            ends_out[rows, :] = leaving[rows, :]
+
+    halves(forward)
+    store(rows_in, rows_in_far)
     store(context, context_far)
-    total[...] = dot(context[...], w_out[...])
-
-    def first_norm(rows):
-        summed = rows_in[rows, :].astype(jnp.float32) + total[rows, :] + vec[2:3, :]
-        normed, inverse = norm_forward(summed)
-        first_normed[rows, :] = normed
-        first_inverse[rows, :] = jnp.broadcast_to(inverse, (STRIP, TILE))
-        shifted = normed * vec[6:7, :] + vec[3:4, :]
-        normed_out[rows, :] = shifted
-        normed_low[rows, :] = shifted.astype(jnp.bfloat16)
-
-    strips(first_norm)
     store(normed_low, normed_low_far)
-    arrived(2)
-    arrived(3)
-
-    def widen(j):
-        columns = slice(j * FF_STEP, (j + 1) * FF_STEP)
-        row, first = j * FF_STEP // WIDTH, j * FF_STEP % WIDTH
-        pre_act = dot(normed_low[...], w_in[:, columns])
-        pre_act = pre_act + vec[8 + row : 9 + row, first : first + FF_STEP]
-        phi = 0.5 * (1.0 + lax.erf(pre_act * 0.7071067811865476))
-        activated[:, columns] = (pre_act * phi).astype(jnp.bfloat16)
-        density = jnp.exp(-0.5 * pre_act * pre_act) * 0.3989422804014327
-        slope[:, columns] = (phi + pre_act * density).astype(jnp.bfloat16)
-
-    for j in range(FF_WIDTH // FF_STEP):
-        widen(j)
-    for n in range(2):
-        columns = slice(n * 512, (n + 1) * 512)
-        total[:, columns] = dot(activated[...], w_down[:, columns])
-
     store(activated, activated_far)
-
-    def second_norm(rows):
-        summed = normed_out[rows, :] + total[rows, :] + vec[4:5, :]
-        normed, inverse = norm_forward(summed)
-        second_normed[rows, :] = normed
-        second_inverse[rows, :] = jnp.broadcast_to(inverse, (STRIP, TILE))
-        leaving[rows, :] = (normed * vec[7:8, :] + vec[5:6, :]).astype(jnp.bfloat16)
-
-    strips(second_norm)
 
     @pl.when(section == 0)
     def _():
-        onward.start()
-        onward.wait_send()
-        back.wait_recv()
-
-    @pl.when(section == 1)
-    def _():
-        ends_out[...] = leaving[...]
+        for n in range(2):
+            passing(n * HALF, rows_in, n).wait_send()
 
     def add_sum(row, values):
         sums[row : row + 1, :] += jnp.sum(values, axis=0, keepdims=True)
 
-    def second_back(rows):
-        grad = cotangent[rows, :].astype(jnp.float32)
-        normed = second_normed[rows, :]
-        add_sum(5, grad)
-        add_sum(7, grad * normed)
-        grad = norm_backward(grad, normed, second_inverse[rows, 0:1], vec[7:8, :])
-        add_sum(4, grad)
-        normed_out[rows, :] = grad
-        second_low[rows, :] = grad.astype(jnp.bfloat16)
-
-    strips(second_back)
-    store(second_low, second_low_far)
-    for j in range(FF_WIDTH // FF_STEP):
-        columns = slice(j * FF_STEP, (j + 1) * FF_STEP)
-        row, first = j * FF_STEP // WIDTH, j * FF_STEP % WIDTH
-        grad = dot_last(second_low[...], w_down[columns, :]) * slope[:, columns].astype(jnp.float32)
-        sums[8 + row : 9 + row, first : first + FF_STEP] = jnp.sum(grad, axis=0, keepdims=True)
-        pre_low[:, columns] = grad.astype(jnp.bfloat16)
-    for n in range(2):
-        columns = slice(n * 512, (n + 1) * 512)
-        total[:, columns] = dot_last(pre_low[...], w_in[columns, :])
-
-    store(pre_low, pre_low_far)
-
-    def first_back(rows):
-        grad = normed_out[rows, :] + total[rows, :]
-        normed = first_normed[rows, :]
-        add_sum(3, grad)
-        add_sum(6, grad * normed)
-        grad = norm_backward(grad, normed, first_inverse[rows, 0:1], vec[6:7, :])
-        add_sum(2, grad)
-        normed_out[rows, :] = grad
-        first_low[rows, :] = grad.astype(jnp.bfloat16)
-
-    strips(first_back)
-    store(first_low, first_low_far)
-    context_grad = leaving
-    for n in range(2):
-        columns = slice(n * 512, (n + 1) * 512)
-        context_grad[:, columns] = dot_last(first_low[...], w_out[columns, :]).astype(jnp.bfloat16)
-
-    def attend_back(p, carry):
-        for b in (0, 1):
-            rows = slice(b * TILE, (b + 1) * TILE)
+    def backward(number, first_row):
+        rows = pl.ds(first_row, HALF)
+
+        @pl.when(section == 0)
+        def _():
+            passing(first_row, cotangent, 2 + number).wait_recv()
+
+        def second_back(rows):
+            grad = cotangent[rows, :].astype(jnp.float32)
+            normed = second_normed[rows, :]
+            add_sum(5, grad)
+            add_sum(7, grad * normed)
+            grad = norm_backward(grad, normed, second_inverse[rows, 0:1], vec[7:8, :])
+            add_sum(4, grad)
+            normed_out[rows, :] = grad
+            second_low[rows, :] = grad.astype(jnp.bfloat16)
+
+        strips(second_back, first_row)
+        for j in range(FF_WIDTH // FF_STEP):
+            columns = slice(j * FF_STEP, (j + 1) * FF_STEP)
+            row, first = j * FF_STEP // WIDTH, j * FF_STEP % WIDTH
+            grad = dot_last(second_low[rows, :], w_down[columns, :]) * slope[rows, columns].astype(jnp.float32)
+            sums[8 + row : 9 + row, first : first + FF_STEP] += jnp.sum(grad, axis=0, keepdims=True)
+            pre_low[rows, columns] = grad.astype(jnp.bfloat16)
+        for n in range(2):
+            columns = slice(n * 512, (n + 1) * 512)
+            total[rows, columns] = dot_last(pre_low[rows, :], w_in[columns, :])
+
+
+        def first_back(rows):
+            grad = normed_out[rows, :] + total[rows, :]
+            normed = first_normed[rows, :]
+            add_sum(3, grad)
+            add_sum(6, grad * normed)
+            grad = norm_backward(grad, normed, first_inverse[rows, 0:1], vec[6:7, :])
+            add_sum(2, grad)
+            normed_out[rows, :] = grad
+            first_low[rows, :] = grad.astype(jnp.bfloat16)
+
+        strips(first_back, first_row)
+        context_grad = leaving
+        for n in range(2):
+            columns = slice(n * 512, (n + 1) * 512)
+            context_grad[rows, columns] = dot_last(first_low[rows, :], w_out[columns, :]).astype(jnp.bfloat16)
+
+        def attend_back(p, carry):
             query = qkv[rows, head_columns(p, 0)]
             key = qkv[rows, head_columns(p, 1)]
             value = qkv[rows, head_columns(p, 2)]
@@ -775,7 +796,7 @@
             results = [0.0, 0.0, 0.0]
             for h in (0, 1):
                 own = grads * head_masks[h]
-                low = chances[p * 4 + b * 2 + h]
+                low = chances[p * 4 + number * 2 + h]
                 share = low.astype(jnp.float32)
                 weight_grad = dot_last(own, value)
                 inner = jnp.sum(share * weight_grad, axis=-1, keepdims=True)
@@ -788,23 +809,27 @@
             for row, part in ((0, 0), (1, 2)):
                 here = head_columns(p, 0)
                 sums[row : row + 1, here] += jnp.sum(results[part], axis=0, keepdims=True)
-        return carry
-
-    lax.fori_loop(0, HEADS // 2, attend_back, 0)
+            return carry
+
+        lax.fori_loop(0, HEADS // 2, attend_back, 0)
+        for n in range(2):
+            columns = slice(n * 512, (n + 1) * 512)
+            grad = normed_out[rows, columns] + dot_last(joined[rows, :], w_qkv[columns, :])
+            leaving[rows, columns] = grad.astype(jnp.bfloat16)
+
+        @pl.when(section == 1)
+        def _():
+            passing(first_row, cotangent, 2 + number).start()
+
+        @pl.when(section == 0)
+        def _():
+            ends_out[rows, :] = leaving[rows, :]
+
+    halves(backward)
     store(joined, joined_far)
-    for n in range(2):
-        columns = slice(n * 512, (n + 1) * 512)
-        grad = normed_out[:, columns] + dot_last(joined[...], w_qkv[columns, :])
-        leaving[:, columns] = grad.astype(jnp.bfloat16)
-
-    @pl.when(section == 1)
-    def _():
-        back.start()
-
-    @pl.when(section == 0)
-    def _():
-        ends_out[...] = leaving[...]
-
+    store(first_low, first_low_far)
+    store(pre_low, pre_low_far)
+    store(second_low, second_low_far)
     for f in range(N_F):
         small_rows[f, 0:8, :] = sums[0:8, f * TILE : (f + 1) * TILE]
         for i in range(4):
@@ -821,7 +846,8 @@
 
     @pl.when(section == 1)
     def _():
-        back.wait_send()
+        for n in range(2):
+            passing(n * HALF, cotangent, 2 + n).wait_send()
 
 
 def run_layer(ends, ids, shards):
@@ -871,8 +897,8 @@
             *[pltpu.VMEM(shape, kind) for shape, kind in scratch],
             pltpu.SemaphoreType.DMA((5,)),
             pltpu.SemaphoreType.DMA((9,)),
-            pltpu.SemaphoreType.DMA((2,)),
-            pltpu.SemaphoreType.DMA((2,)),
+            pltpu.SemaphoreType.DMA((4,)),
+            pltpu.SemaphoreType.DMA((4,)),
             pltpu.SemaphoreType.DMA((GATHER_COPIES,)),
             pltpu.SemaphoreType.DMA((GATHER_COPIES,)),
         ],

time: 290 us -> 282 us (0.972)
  Pallas kernels: 284 us -> 276 us
    pallas_call x1, Pallas kernels: 166 us -> 159 us  [run_layer(): pl.pallas_call(layer_kernel, out_shape=[jax.ShapeDtypeStruct((ROWS, WIDTH...]
where the time goes in v5:
time: 282 us
  Pallas kernels  276 us (98%)
  local copies, waits for them, and re-layouts  2.87 us (1%)
    pallas_call x1, Pallas kernels, run_layer(): pl.pallas_call(layer_kernel, out_shape=[jax.ShapeDtypeStruct((ROWS, WIDTH...  159 us
    pallas_call x1, Pallas kernels, reduce_grads(): pl.pallas_call(reduce_kernel, out_shape=jax.ShapeDtypeStruct((TILE, PAYLO...  112 us

profile of v5, /device:TPU:6, one launch (start us, length us, event | category | flops | bytes accessed | tf_op | source)
XLA Modules:
  0.0 282.2 jit_solution(7529049911775184689)
XLA Ops:
  0.6 0.7 fusion.10
  1.3 0.0 copy-start.1
  1.3 0.7 reduce
  2.0 1.3 fusion.8.small_shard
  3.3 0.8 copy.18.id_column
  4.1 0.0 copy-done.1
  4.1 158.7 %run_layer.1 = (bf16[256,1024]{1,0:T(8,128)(2,1)}, bf16[256,1024]{1,0:T(8,128)(2,1)}, bf16[256,1024]{1,0:T(8,128)(2,1)}, bf16[256,1024]{1,0:T(8,128)(2,1)}, bf16...) custom-call(bf16[256,1024]{1,0:T(8,128)(2,1)} %bitcast.22, ...), custom_call_target="tpu_custom_call" | custom-call | tf_op jit(solution)/shard_map/run_layer/pallas_call | solution.py:887
  162.9 112.1 %reduce_grads.1.low = bf16[128,12416]{1,0:T(8,128)(2,1)} custom-call(bf16[256,1024]{1,0:T(8,128)(2,1)} %get-tuple-element.26.refs_0_, bf16[256,1024]{1,0:T(8,128)(2,1)} %get-tuple-element.27.refs_1_, bf16[256,1024]{1,0:T(8,128)(2,1)} %get-tuple-element.28.refs_2_, bf16[256,4096]{1,0:T(8,128)(2,1)} %get-tuple-element.29.refs_3_, ...), custom_call_target="tpu_custom_call" | custom-call | tf_op jit(solution)/shard_map/reduce_grads/pallas_call | solution.py:455
  275.0 0.0 copy-start
  275.0 5.1 %widen_outputs.1 = (f32[128,3072]{1,0:T(8,128)}, f32[128,1024]{1,0:T(8,128)}, f32[128,4096]{1,0:T(8,128)}, f32[4,128,1024]{2,1,0:T(8,128)}, f32[6,128]{1,0:T(8,1...) custom-call(bf16[128,12416]{1,0:T(8,128)(2,1)} %reduce_grads.1.low), custom_call_target="tpu_custom_call" | custom-call | tf_op jit(solution)/shard_map/widen_outputs/pallas_call | solution.py:500
  280.1 1.3 copy.19
  281.4 0.0 copy-done
  281.4 0.8 copy.21
Async XLA Ops:
  1.3 2.8 copy-start.1
  275.0 6.4 %copy-start = (bf16[256,1024]{1,0:T(8,128)(2,1)S(1)}, bf16[256,1024]{1,0:T(8,128)(2,1)}, u32[]{:S(2)}) copy-start(bf16[256,1024]{1,0:T(8,128)(2,1)} %get-tuple-element.25) | copy-start | bytes 1572868

commit v6 on v5

--- a/solution.py
+++ b/solution.py
@@ -175,22 +175,32 @@
         send_on("direct", k)
     for k in relayed:
         send_further(2, k)
-    for k in range(count):
-        for n in range(3):
-            if n == 2 and k in direct:
-                second_right["direct", k].wait_recv()
-                second_left["direct", k].wait_recv()
-            if k in relayed:
-                further[n, k, 0].wait_recv()
-                further[n, k, 1].wait_recv()
-            block = span(k, owners[n], 0, GATHER_PLAN[k][0])
-            sibling_copies[n, k] = copies.start(block, block, sibling)
+    def pass_on(n, k):
+        if n == 2 and k in direct:
+            second_right["direct", k].wait_recv()
+            second_left["direct", k].wait_recv()
+        if k in relayed:
+            further[n, k, 0].wait_recv()
+            further[n, k, 1].wait_recv()
+        block = span(k, owners[n], 0, GATHER_PLAN[k][0])
+        sibling_copies[n, k] = copies.start(block, block, sibling)
+
+    order = (4, 0, 1, 2, 3)
+    for n in (0, 1):
+        for k in order:
+            pass_on(n, k)
+    pass_on(2, 4)
+    pass_on(2, 0)
+
+    def finish():
+        for k in order[2:]:
+            pass_on(2, k)
 
     def arrived(k):
         for n in range(4):
             sibling_copies[n, k].wait_recv()
 
-    return arrived
+    return arrived, finish
 
 
 REDUCE_PLAN = tuple(
@@ -596,7 +606,7 @@
     section = lax.axis_index("section")
     other = {"section": 1 - section}
     copies = Copies(gather_send_sem, gather_recv_sem)
-    arrived = gather_into(
+    arrived, finish = gather_into(
         (w_qkv_shard, w_out_shard, w_in_shard, w_down_shard, small_shard),
         (w_qkv, w_out, w_in, w_down, small),
         copies,
@@ -642,18 +652,11 @@
     def _():
         cotangent[...] = ends[...]
 
-    for k in range(4):
-        arrived(k)
+    arrived(0)
     def head_columns(p, part):
         return pl.ds(pl.multiple_of(part * WIDTH + p * TILE, TILE), TILE)
 
-    def forward(number, first_row):
-        rows = pl.ds(first_row, HALF)
-
-        @pl.when(section == 1)
-        def _():
-            passing(first_row, rows_in, number).wait_recv()
-
+    def project(rows):
         for j in range(6):
             columns = slice(j * 512, (j + 1) * 512)
             projected = dot(rows_in[rows, :], w_qkv[:, columns])
@@ -663,6 +666,7 @@
                 projected = projected + vec[row : row + 1, first : first + 512]
             qkv[rows, columns] = projected.astype(jnp.bfloat16)
 
+    def mix(number, rows):
         def attend(p, carry):
             query = qkv[rows, head_columns(p, 0)]
             key = qkv[rows, head_columns(p, 1)]
@@ -682,6 +686,29 @@
             return carry
 
         lax.fori_loop(0, HEADS // 2, attend, 0)
+
+    @pl.when(section == 0)
+    def _():
+        project(slice(0, ROWS))
+
+    finish()
+
+    @pl.when(section == 0)
+    def _():
+        halves(lambda number, first_row: mix(number, pl.ds(first_row, HALF)))
+
+    for k in (1, 2, 3):
+        arrived(k)
+
+    def forward(number, first_row):
+        rows = pl.ds(first_row, HALF)
+
+        @pl.when(section == 1)
+        def _():
+            passing(first_row, rows_in, number).wait_recv()
+            project(rows)
+            mix(number, rows)
+
         total[rows, :] = dot(context[rows, :], w_out[...])
 
         def first_norm(rows):

time: 282 us -> 278 us (0.986)
  Pallas kernels: 276 us -> 271 us
    pallas_call x1, Pallas kernels: 159 us -> 153 us  [run_layer(): pl.pallas_call(layer_kernel, out_shape=[jax.ShapeDtypeStruct((ROWS, WIDTH...]
where the time goes in v6:
time: 278 us; the launch traced here: 277 us
  Pallas kernels  271 us (97%)
  local copies, waits for them, and re-layouts  2.87 us (1%)
    pallas_call x1, Pallas kernels, run_layer(): pl.pallas_call(layer_kernel, out_shape=[jax.ShapeDtypeStruct((ROWS, WIDTH...  153 us
    pallas_call x1, Pallas kernels, reduce_grads(): pl.pallas_call(reduce_kernel, out_shape=jax.ShapeDtypeStruct((TILE, PAYLO...  113 us

profile of v6, /device:TPU:6, one launch (start us, length us, event | category | flops | bytes accessed | tf_op | source)
XLA Modules:
  0.0 277.2 jit_solution(17913047245971708810)
XLA Ops:
  0.6 0.7 fusion.10
  1.3 0.0 copy-start.1
  1.3 0.7 reduce
  2.0 1.3 fusion.8.small_shard
  3.3 0.8 copy.18.id_column
  4.1 0.0 copy-done.1
  4.1 153.3 %run_layer.1 = (bf16[256,1024]{1,0:T(8,128)(2,1)}, bf16[256,1024]{1,0:T(8,128)(2,1)}, bf16[256,1024]{1,0:T(8,128)(2,1)}, bf16[256,1024]{1,0:T(8,128)(2,1)}, bf16...) custom-call(bf16[256,1024]{1,0:T(8,128)(2,1)} %bitcast.22, ...), custom_call_target="tpu_custom_call" | custom-call | tf_op jit(solution)/shard_map/run_layer/pallas_call | solution.py:914
  157.5 112.5 %reduce_grads.1.low = bf16[128,12416]{1,0:T(8,128)(2,1)} custom-call(bf16[256,1024]{1,0:T(8,128)(2,1)} %get-tuple-element.26.refs_0_, bf16[256,1024]{1,0:T(8,128)(2,1)} %get-tuple-element.27.refs_1_, bf16[256,1024]{1,0:T(8,128)(2,1)} %get-tuple-element.28.refs_2_, bf16[256,4096]{1,0:T(8,128)(2,1)} %get-tuple-element.29.refs_3_, ...), custom_call_target="tpu_custom_call" | custom-call | tf_op jit(solution)/shard_map/reduce_grads/pallas_call | solution.py:465
  270.0 0.0 copy-start
  270.0 5.1 %widen_outputs.1 = (f32[128,3072]{1,0:T(8,128)}, f32[128,1024]{1,0:T(8,128)}, f32[128,4096]{1,0:T(8,128)}, f32[4,128,1024]{2,1,0:T(8,128)}, f32[6,128]{1,0:T(8,1...) custom-call(bf16[128,12416]{1,0:T(8,128)(2,1)} %reduce_grads.1.low), custom_call_target="tpu_custom_call" | custom-call | tf_op jit(solution)/shard_map/widen_outputs/pallas_call | solution.py:510
  275.1 1.3 copy.19
  276.4 0.0 copy-done
  276.4 0.8 copy.21
Async XLA Ops:
  1.3 2.8 %copy-start.1 = (s32[256]{0:T(256)}, s32[256]{0:T(256)S(1)}, u32[]{:S(2)}) copy-start(s32[256]{0:T(256)S(1)} %fusion.10) | copy-start | bytes 3076
  270.0 6.4 %copy-start = (bf16[256,1024]{1,0:T(8,128)(2,1)S(1)}, bf16[256,1024]{1,0:T(8,128)(2,1)}, u32[]{:S(2)}) copy-start(bf16[256,1024]{1,0:T(8,128)(2,1)} %get-tuple-element.25) | copy-start | bytes 1572868

commit v7 on v6

--- a/solution.py
+++ b/solution.py
@@ -162,7 +162,7 @@
         send_on("relay", k)
         send_along(0, k)
         send_along(1, k)
-    for k in direct[::-1]:
+    for k in (4, 0, 1, 2):
         send_own("direct", k)
     for k in relayed:
         second_right["relay", k].wait_recv()
@@ -171,7 +171,7 @@
     for n in (0, 1):
         for k in relayed:
             send_further(n, k)
-    for k in direct[::-1]:
+    for k in (4, 0, 1, 2):
         send_on("direct", k)
     for k in relayed:
         send_further(2, k)

time: 278 us -> 278 us (level)
  no operation moved by 1% of the time
where the time goes in v7:
time: 278 us; the launch traced here: 277 us
  Pallas kernels  271 us (97%)
  local copies, waits for them, and re-layouts  2.87 us (1%)
    pallas_call x1, Pallas kernels, run_layer(): pl.pallas_call(layer_kernel, out_shape=[jax.ShapeDtypeStruct((ROWS, WIDTH...  153 us
    pallas_call x1, Pallas kernels, reduce_grads(): pl.pallas_call(reduce_kernel, out_shape=jax.ShapeDtypeStruct((TILE, PAYLO...  113 us

profile of v7, /device:TPU:6, one launch (start us, length us, event | category | flops | bytes accessed | tf_op | source)
XLA Modules:
  0.0 277.2 jit_solution(1288297056437808741)
XLA Ops:
  0.6 0.7 fusion.10
  1.3 0.0 copy-start.1
  1.3 0.7 reduce
  2.0 1.3 fusion.8.small_shard
  3.3 0.8 copy.18.id_column
  4.1 0.0 copy-done.1
  4.1 153.3 %run_layer.1 = (bf16[256,1024]{1,0:T(8,128)(2,1)}, bf16[256,1024]{1,0:T(8,128)(2,1)}, bf16[256,1024]{1,0:T(8,128)(2,1)}, bf16[256,1024]{1,0:T(8,128)(2,1)}, bf16...) custom-call(bf16[256,1024]{1,0:T(8,128)(2,1)} %bitcast.22, ...), custom_call_target="tpu_custom_call" | custom-call | tf_op jit(solution)/shard_map/run_layer/pallas_call | solution.py:914
  157.5 112.5 %reduce_grads.1.low = bf16[128,12416]{1,0:T(8,128)(2,1)} custom-call(bf16[256,1024]{1,0:T(8,128)(2,1)} %get-tuple-element.26.refs_0_, bf16[256,1024]{1,0:T(8,128)(2,1)} %get-tuple-element.27.refs_1_, bf16[256,1024]{1,0:T(8,128)(2,1)} %get-tuple-element.28.refs_2_, bf16[256,4096]{1,0:T(8,128)(2,1)} %get-tuple-element.29.refs_3_, ...), custom_call_target="tpu_custom_call" | custom-call | tf_op jit(solution)/shard_map/reduce_grads/pallas_call | solution.py:465
  270.0 0.0 copy-start
  270.0 5.1 %widen_outputs.1 = (f32[128,3072]{1,0:T(8,128)}, f32[128,1024]{1,0:T(8,128)}, f32[128,4096]{1,0:T(8,128)}, f32[4,128,1024]{2,1,0:T(8,128)}, f32[6,128]{1,0:T(8,1...) custom-call(bf16[128,12416]{1,0:T(8,128)(2,1)} %reduce_grads.1.low), custom_call_target="tpu_custom_call" | custom-call | tf_op jit(solution)/shard_map/widen_outputs/pallas_call | solution.py:510
  275.1 1.3 copy.19
  276.4 0.0 copy-done
  276.4 0.8 copy.21
Async XLA Ops:
  1.3 2.8 %copy-start.1 = (s32[256]{0:T(256)}, s32[256]{0:T(256)S(1)}, u32[]{:S(2)}) copy-start(s32[256]{0:T(256)S(1)} %fusion.10) | copy-start | bytes 3076
  270.0 6.4 %copy-start = (bf16[256,1024]{1,0:T(8,128)(2,1)S(1)}, bf16[256,1024]{1,0:T(8,128)(2,1)}, u32[]{:S(2)}) copy-start(bf16[256,1024]{1,0:T(8,128)(2,1)} %get-tuple-element.25) | copy-start | bytes 1572868
